TPU v7x, 256 devices: a whole 4x4x8 slice. The times are simulated.
256 devices in a mesh: pole: 4 (over x), row: 16 (over z, core), col: 4 (over y).
Axes of the slice: x: 4, y: 4, z: 8, core: 2. Of those that a mesh axis runs over, the one named last changes fastest.
Arguments:
- lower_one: bfloat16 [4, 2, 1, 1024, 1024], P('pole', None, None, 'row', 'col'), may hold values from -0.125 to 0.125
- lower_two: bfloat16 [4, 4, 2, 1024, 1024], P('pole', None, None, 'row', 'col'), may hold values from -0.09375 to 0.09375
- lower_three: bfloat16 [4, 8, 3, 1024, 1024], P('pole', None, None, 'row', 'col'), may hold values from -0.078125 to 0.078125
- diag_inverse: bfloat16 [4, 15, 1024, 1024], P('pole', None, 'row', 'col'), as said below
- pole_weight: float32 [4], P('pole'), may hold values from 0.3 to 3
- super_sizes: int32 [15, 2], replicated, may hold values from 128 to 512, as said below
- parents: int32 [12], replicated, may hold values from 0 to 3, as said below
- keep_two: int32 [4], replicated, may hold values 0 or 1
- keep_three: int32 [8, 2], replicated, may hold values 0 or 1
Outputs:
- density_top: float32 [5, 1024, 1024], P(None, 'row', 'col')
- density_two: float32 [4, 3, 1024, 1024], P('pole', None, 'row', 'col')
- density_three: float32 [8, 4, 1024, 1024], P('pole', None, 'row', 'col')
Inputs may be any that keep to these rules, and one draw needn't show every extreme that they name: `super_sizes`: each tree node's block of 1024 rows holds 2 supernodes of up to 512 rows each; the largest and the smallest size occur in every draw. `parents`: entries 0 to 3 each lie in 0 to 1, and each level-one node is named by exactly two of them; entries 4 to 11 each lie in 0 to 3, and each level-two node is named by exactly two of them. Each block diag_inverse[p, k] is symmetric.
All inputs are finite; a program needn't handle non-finite values.
Results may differ from a plain program's by a relative error of at most 0.0035.
Values may be sent and summed in bfloat16 or wider, within the bound.
A program may use at most 128 MiB of HBM per device.

v0:
```python
import jax
import jax.numpy as jnp
from jax import lax
from jax.sharding import PartitionSpec as P

SUPB = 512
NSUP = 2


def live_table(super_sizes):
    places = jnp.arange(SUPB, dtype=jnp.int32)
    node_count = super_sizes.shape[0]
    return (
        (places[None, None, :] < super_sizes[:, :, None])
        .reshape(node_count, NSUP * SUPB)
        .astype(jnp.bfloat16)
    )


def full_rows(blocks):
    return lax.all_gather(blocks, "col", axis=2, tiled=True)


def descend(panels, factor, dinv_blocks, extend):
    node_count = factor.shape[0]
    depth = factor.shape[1]
    columns = lax.all_gather(factor, "row", axis=2, tiled=True)
    full_width = columns.shape[2]
    flat = columns.reshape(node_count, depth * full_width, columns.shape[3])
    inverse = -jnp.einsum("xmik,xkj->xmij", panels, flat, preferred_element_type=jnp.float32)
    inverse = inverse.astype(jnp.bfloat16)
    inverse_rows = lax.all_gather(inverse, "col", axis=3, tiled=True)
    inverse_cols = lax.all_to_all(inverse_rows, "row", split_axis=3, concat_axis=2, tiled=True)
    product = jnp.einsum(
        "xmia,xmij->xaj", inverse_cols, columns, preferred_element_type=jnp.float32
    )
    diagonal = (dinv_blocks.astype(jnp.float32) - product).astype(jnp.bfloat16)
    if not extend:
        return (inverse, diagonal, None)
    diagonal_full = full_rows(diagonal)
    upper = jnp.concatenate([panels, inverse_rows], axis=3)
    turned = jnp.swapaxes(inverse_cols, 2, 3)
    lower = jnp.concatenate(
        [turned[:, position] for position in range(depth)] + [diagonal_full], axis=2
    )
    return (inverse, diagonal, jnp.concatenate([upper, lower[:, None]], axis=1))


def sweep(paths, parent_list, factor, dinv_blocks, extend):
    results = []
    for position in range(factor.shape[0]):
        panels = jnp.take(paths, parent_list[position : position + 1], axis=0)
        results.append(
            descend(
                panels,
                factor[position : position + 1],
                dinv_blocks[position : position + 1],
                extend,
            )
        )
    inverse = jnp.concatenate([result[0] for result in results], axis=0)
    diagonal = jnp.concatenate([result[1] for result in results], axis=0)
    if not extend:
        return (inverse, diagonal, None)
    return (inverse, diagonal, jnp.concatenate([result[2] for result in results], axis=0))


def local(
    lower_one,
    lower_two,
    lower_three,
    diag_inverse,
    pole_weight,
    super_sizes,
    parents,
    keep_two,
    keep_three,
):
    full_width = NSUP * SUPB
    row_count = full_width // lax.axis_size("row")
    col_count = full_width // lax.axis_size("col")
    parent_two = parents[0:4]
    parent_three = parents[4:12]
    live_mask = live_table(super_sizes)
    live_rows = lax.dynamic_slice_in_dim(live_mask, lax.axis_index("row") * row_count, row_count, 1)
    live_cols = lax.dynamic_slice_in_dim(live_mask, lax.axis_index("col") * col_count, col_count, 1)
    grand_parent = jnp.take(parent_two, parent_three)
    root_parents = jnp.zeros((2,), jnp.int32)
    rows_one = live_rows[0][None, None, :]
    rows_two = jnp.stack(
        [
            live_rows[0][None, :] * keep_two[:, None].astype(jnp.bfloat16),
            jnp.take(live_rows, 1 + parent_two, axis=0),
        ],
        axis=1,
    )
    rows_three = jnp.stack(
        [
            live_rows[0][None, :] * keep_three[:, 0:1].astype(jnp.bfloat16),
            jnp.take(live_rows, 1 + grand_parent, axis=0) * keep_three[:, 1:2].astype(jnp.bfloat16),
            jnp.take(live_rows, 3 + parent_three, axis=0),
        ],
        axis=1,
    )
    dinv_blocks = diag_inverse[0] * live_rows[:, :, None] * live_cols[:, None, :]
    root_panel = full_rows(dinv_blocks[0:1])[:, None]
    factor_one = lower_one[0] * rows_one[:, :, :, None] * live_cols[1:3][:, None, None, :]
    inverse_one, diagonal_one, paths_one = sweep(
        root_panel, root_parents, factor_one, dinv_blocks[1:3], True
    )
    factor_two = lower_two[0] * rows_two[:, :, :, None] * live_cols[3:7][:, None, None, :]
    inverse_two, diagonal_two, paths_two = sweep(
        paths_one, parent_two, factor_two, dinv_blocks[3:7], True
    )
    factor_three = lower_three[0] * rows_three[:, :, :, None] * live_cols[7:15][:, None, None, :]
    inverse_three, diagonal_three, unused = sweep(
        paths_two, parent_three, factor_three, dinv_blocks[7:15], False
    )
    weight = pole_weight[0]
    level_one = jnp.concatenate([inverse_one, diagonal_one[:, None]], axis=1).reshape(
        4, row_count, col_count
    )
    top_terms = jnp.concatenate([dinv_blocks[0:1], level_one], axis=0)
    top_sum = weight * top_terms.astype(jnp.float32)
    two_sum = weight * jnp.concatenate([inverse_two, diagonal_two[:, None]], axis=1).astype(
        jnp.float32
    )
    three_sum = weight * jnp.concatenate([inverse_three, diagonal_three[:, None]], axis=1).astype(
        jnp.float32
    )
    density_top = lax.psum(top_sum, "pole")
    density_two, density_three = (
        lax.psum_scatter(two_sum, "pole", scatter_dimension=0, tiled=True),
        lax.psum_scatter(three_sum, "pole", scatter_dimension=0, tiled=True),
    )
    return (density_top, density_two, density_three)


def solution(mesh):
    placed = (
        P("pole", None, None, "row", "col"),
        P("pole", None, None, "row", "col"),
        P("pole", None, None, "row", "col"),
        P("pole", None, "row", "col"),
        P("pole"),
        P(),
        P(),
        P(),
        P(),
    )
    return jax.shard_map(
        local,
        mesh=mesh,
        in_specs=placed,
        out_specs=(
            P(None, "row", "col"),
            P("pole", None, "row", "col"),
            P("pole", None, "row", "col"),
        ),
        check_vma=False,
    )
```

profile of v0, /device:TPU:1, one launch (start us, length us, event | category | flops | bytes accessed | tf_op | source)
XLA Modules:
  0.0 639.5 jit_solution(2522528278018070078)
XLA Ops:
  22.0 11.0 %all_gather.105 = bf16[1,64,1024]{2,1,0:T(8,128)(2,1)S(1)} all-gather(bf16[1,64,256]{2,1,0:T(8,128)(2,1)S(1)} %slice.292), channel_id=1, replica_groups=mesh['pole'=4,'row'=16,'col'=4] {'col'}, dimensions={2}, use_global_device_ids=true | all-gather | bytes 163840 | tf_op jit(solution)/shard_map/all_gather | solution.py:21
  33.1 24.3 %all_gather.107 = bf16[1,1,1024,256]{3,2,0,1:T(8,128)(2,1)S(1)} all-gather(bf16[1,1,64,256]{3,2,0,1:T(8,128)(2,1)S(1)} %get-tuple-element.59), channel_id=1, replica_groups=mesh['pole'=4,'row'=16,'col'=4] {'row'}, dimensions={2}, use_global_device_ids=true | all-gather | bytes 557056 | tf_op jit(solution)/shard_map/all_gather | solution.py:27
  57.6 9.5 %all-gather.1 = bf16[64,1024]{1,0:T(8,128)(2,1)S(1)} all-gather(bf16[64,256]{1,0:T(8,128)(2,1)S(1)} %fusion.167), channel_id=3, replica_groups=mesh['pole'=4,'row'=16,'col'=4] {'col'}, dimensions={1}, use_global_device_ids=true | all-gather | bytes 163840 | tf_op jit(solution)/shard_map/all_gather | solution.py:32
  78.0 19.5 %all_gather.106 = bf16[1,1,1024,256]{3,2,0,1:T(8,128)(2,1)S(1)} all-gather(bf16[1,1,64,256]{3,2,0,1:T(8,128)(2,1)S(1)} %get-tuple-element.58), channel_id=1, replica_groups=mesh['pole'=4,'row'=16,'col'=4] {'row'}, dimensions={2}, use_global_device_ids=true | all-gather | bytes 557056 | tf_op jit(solution)/shard_map/all_gather | solution.py:27
  97.7 9.1 %all-gather = bf16[64,1024]{1,0:T(8,128)(2,1)S(1)} all-gather(bf16[64,256]{1,0:T(8,128)(2,1)S(1)} %fusion.166), channel_id=2, replica_groups=mesh['pole'=4,'row'=16,'col'=4] {'col'}, dimensions={1}, use_global_device_ids=true | all-gather | bytes 163840 | tf_op jit(solution)/shard_map/all_gather | solution.py:32
  110.5 9.1 %all-to-all-start = ((bf16[16,2,2048]{2,1,0:T(2,128)(2,1)}), bf16[16,2,2048]{2,1,0:T(2,128)(2,1)S(1)}, u32[]{:S(2)}, u32[]{:S(2)}) async-start(bf16[16,2,2048]{2,1,0:T(2,128)(2,1)} %reshape.765), calls=%async_computation | async-start | bytes 262144 | tf_op jit(solution)/shard_map/all_to_all | solution.py:33
  132.3 9.5 %all_gather.111 = bf16[1,64,1024]{2,1,0:T(8,128)(2,1)S(1)} all-gather(bf16[1,64,256]{2,1,0:T(8,128)(2,1)S(1)} %fusion.169), channel_id=1, replica_groups=mesh['pole'=4,'row'=16,'col'=4] {'col'}, dimensions={2}, use_global_device_ids=true | all-gather | bytes 163840 | tf_op jit(solution)/shard_map/all_gather | solution.py:21
  141.7 9.5 %all_gather.110 = bf16[1,64,1024]{2,1,0:T(8,128)(2,1)S(1)} all-gather(bf16[1,64,256]{2,1,0:T(8,128)(2,1)S(1)} %fusion.168), channel_id=1, replica_groups=mesh['pole'=4,'row'=16,'col'=4] {'col'}, dimensions={2}, use_global_device_ids=true | all-gather | bytes 163840 | tf_op jit(solution)/shard_map/all_gather | solution.py:21
  153.2 9.6 %all-gather.5 = bf16[2,64,1024]{2,1,0:T(8,128)(2,1)S(1)} all-gather(bf16[2,64,256]{2,1,0:T(8,128)(2,1)S(1)} %fusion.107), channel_id=7, replica_groups=mesh['pole'=4,'row'=16,'col'=4] {'col'}, dimensions={2}, use_global_device_ids=true | all-gather | bytes 327680 | tf_op jit(solution)/shard_map/all_gather | solution.py:32
  164.3 14.9 %all-to-all-start.5 = ((bf16[16,2,4096]{2,1,0:T(2,128)(2,1)}), bf16[16,2,4096]{2,1,0:T(2,128)(2,1)S(1)}, u32[]{:S(2)}, u32[]{:S(2)}) async-start(bf16[16,2,4096]{2,1,0:T(2,128)(2,1)} %reshape.767), calls=%async_computation.5 | async-start | bytes 524288 | tf_op jit(solution)/shard_map/all_to_all | solution.py:33
  180.7 10.4 %all-gather.4 = bf16[2,64,1024]{2,1,0:T(8,128)(2,1)S(1)} all-gather(bf16[2,64,256]{2,1,0:T(8,128)(2,1)S(1)} %fusion.106), channel_id=6, replica_groups=mesh['pole'=4,'row'=16,'col'=4] {'col'}, dimensions={2}, use_global_device_ids=true | all-gather | bytes 327680 | tf_op jit(solution)/shard_map/all_gather | solution.py:32
  192.6 9.1 %all-to-all-start.4 = ((bf16[16,2,4096]{2,1,0:T(2,128)(2,1)}), bf16[16,2,4096]{2,1,0:T(2,128)(2,1)}, u32[]{:S(2)}, u32[]{:S(2)}) async-start(bf16[16,2,4096]{2,1,0:T(2,128)(2,1)} %reshape.769), calls=%async_computation.4 | async-start | bytes 524288 | tf_op jit(solution)/shard_map/all_to_all | solution.py:33
  203.3 10.6 %all-gather.3 = bf16[2,64,1024]{2,1,0:T(8,128)(2,1)S(1)} all-gather(bf16[2,64,256]{2,1,0:T(8,128)(2,1)S(1)} %fusion.105), channel_id=5, replica_groups=mesh['pole'=4,'row'=16,'col'=4] {'col'}, dimensions={2}, use_global_device_ids=true | all-gather | bytes 327680 | tf_op jit(solution)/shard_map/all_gather | solution.py:32
  226.5 10.6 %all-gather.2 = bf16[2,64,1024]{2,1,0:T(8,128)(2,1)S(1)} all-gather(bf16[2,64,256]{2,1,0:T(8,128)(2,1)S(1)} %fusion.104), channel_id=4, replica_groups=mesh['pole'=4,'row'=16,'col'=4] {'col'}, dimensions={2}, use_global_device_ids=true | all-gather | bytes 327680 | tf_op jit(solution)/shard_map/all_gather | solution.py:32
  240.4 9.0 %all-to-all-start.2 = ((bf16[16,2,4096]{2,1,0:T(2,128)(2,1)}), bf16[16,2,4096]{2,1,0:T(2,128)(2,1)}, u32[]{:S(2)}, u32[]{:S(2)}) async-start(bf16[16,2,4096]{2,1,0:T(2,128)(2,1)} %reshape.773), calls=%async_computation.2 | async-start | bytes 524288 | tf_op jit(solution)/shard_map/all_to_all | solution.py:33
  275.3 10.0 %all_gather.123 = bf16[1,64,1024]{2,1,0:T(8,128)(2,1)S(1)} all-gather(bf16[1,64,256]{2,1,0:T(8,128)(2,1)S(1)} %fusion.162), channel_id=1, replica_groups=mesh['pole'=4,'row'=16,'col'=4] {'col'}, dimensions={2}, use_global_device_ids=true | all-gather | bytes 163840 | tf_op jit(solution)/shard_map/all_gather | solution.py:21
  286.7 9.6 %all_gather.122 = bf16[1,64,1024]{2,1,0:T(8,128)(2,1)S(1)} all-gather(bf16[1,64,256]{2,1,0:T(8,128)(2,1)S(1)} %fusion.163), channel_id=1, replica_groups=mesh['pole'=4,'row'=16,'col'=4] {'col'}, dimensions={2}, use_global_device_ids=true | all-gather | bytes 163840 | tf_op jit(solution)/shard_map/all_gather | solution.py:21
  296.7 9.1 %all_gather.121 = bf16[1,64,1024]{2,1,0:T(8,128)(2,1)S(1)} all-gather(bf16[1,64,256]{2,1,0:T(8,128)(2,1)S(1)} %fusion.164), channel_id=1, replica_groups=mesh['pole'=4,'row'=16,'col'=4] {'col'}, dimensions={2}, use_global_device_ids=true | all-gather | bytes 163840 | tf_op jit(solution)/shard_map/all_gather | solution.py:21
  306.2 9.1 %all_gather.120 = bf16[1,64,1024]{2,1,0:T(8,128)(2,1)S(1)} all-gather(bf16[1,64,256]{2,1,0:T(8,128)(2,1)S(1)} %fusion.165), channel_id=1, replica_groups=mesh['pole'=4,'row'=16,'col'=4] {'col'}, dimensions={2}, use_global_device_ids=true | all-gather | bytes 163840 | tf_op jit(solution)/shard_map/all_gather | solution.py:21
  322.8 21.0 %all-gather.6 = bf16[3,64,1024]{2,1,0:T(8,128)(2,1)S(1)} all-gather(bf16[3,64,256]{2,1,0:T(8,128)(2,1)S(1)} %get-tuple-element.77), channel_id=8, replica_groups=mesh['pole'=4,'row'=16,'col'=4] {'col'}, dimensions={2}, use_global_device_ids=true | all-gather | bytes 491520 | tf_op jit(solution)/shard_map/all_gather | solution.py:32
  345.9 20.6 %all-to-all-start.6 = ((bf16[16,2,6144]{2,1,0:T(2,128)(2,1)}), bf16[16,2,6144]{2,1,0:T(2,128)(2,1)S(1)}, u32[]{:S(2)}, u32[]{:S(2)}) async-start(bf16[16,2,6144]{2,1,0:T(2,128)(2,1)} %reshape.775), calls=%async_computation.7 | async-start | bytes 786432 | tf_op jit(solution)/shard_map/all_to_all | solution.py:33
  371.7 10.4 %all-gather.7 = bf16[3,64,1024]{2,1,0:T(8,128)(2,1)S(1)} all-gather(bf16[3,64,256]{2,1,0:T(8,128)(2,1)S(1)} %get-tuple-element.79), channel_id=9, replica_groups=mesh['pole'=4,'row'=16,'col'=4] {'col'}, dimensions={2}, use_global_device_ids=true | all-gather | bytes 491520 | tf_op jit(solution)/shard_map/all_gather | solution.py:32
  384.3 9.3 %all-to-all-start.7 = ((bf16[16,2,6144]{2,1,0:T(2,128)(2,1)}), bf16[16,2,6144]{2,1,0:T(2,128)(2,1)S(1)}, u32[]{:S(2)}, u32[]{:S(2)}) async-start(bf16[16,2,6144]{2,1,0:T(2,128)(2,1)} %reshape.777), calls=%async_computation.8 | async-start | bytes 786432 | tf_op jit(solution)/shard_map/all_to_all | solution.py:33
  398.7 11.1 %all-gather.8 = bf16[3,64,1024]{2,1,0:T(8,128)(2,1)S(1)} all-gather(bf16[3,64,256]{2,1,0:T(8,128)(2,1)S(1)} %get-tuple-element.81), channel_id=10, replica_groups=mesh['pole'=4,'row'=16,'col'=4] {'col'}, dimensions={2}, use_global_device_ids=true | all-gather | bytes 491520 | tf_op jit(solution)/shard_map/all_gather | solution.py:32
  425.2 11.2 %all-gather.9 = bf16[3,64,1024]{2,1,0:T(8,128)(2,1)S(1)} all-gather(bf16[3,64,256]{2,1,0:T(8,128)(2,1)S(1)} %get-tuple-element.83), channel_id=11, replica_groups=mesh['pole'=4,'row'=16,'col'=4] {'col'}, dimensions={2}, use_global_device_ids=true | all-gather | bytes 491520 | tf_op jit(solution)/shard_map/all_gather | solution.py:32
  452.1 12.0 %all-gather.10 = bf16[3,64,1024]{2,1,0:T(8,128)(2,1)} all-gather(bf16[3,64,256]{2,1,0:T(8,128)(2,1)S(1)} %get-tuple-element.85), channel_id=12, replica_groups=mesh['pole'=4,'row'=16,'col'=4] {'col'}, dimensions={2}, use_global_device_ids=true | all-gather | bytes 491520 | tf_op jit(solution)/shard_map/all_gather | solution.py:32
  483.2 11.3 %all-gather.11 = bf16[3,64,1024]{2,1,0:T(8,128)(2,1)S(1)} all-gather(bf16[3,64,256]{2,1,0:T(8,128)(2,1)S(1)} %get-tuple-element.87), channel_id=13, replica_groups=mesh['pole'=4,'row'=16,'col'=4] {'col'}, dimensions={2}, use_global_device_ids=true | all-gather | bytes 491520 | tf_op jit(solution)/shard_map/all_gather | solution.py:32
  509.3 11.6 %all-gather.12 = bf16[3,64,1024]{2,1,0:T(8,128)(2,1)} all-gather(bf16[3,64,256]{2,1,0:T(8,128)(2,1)S(1)} %get-tuple-element.89), channel_id=14, replica_groups=mesh['pole'=4,'row'=16,'col'=4] {'col'}, dimensions={2}, use_global_device_ids=true | all-gather | bytes 491520 | tf_op jit(solution)/shard_map/all_gather | solution.py:32
  524.0 9.2 %all-to-all-start.12 = ((bf16[16,2,6144]{2,1,0:T(2,128)(2,1)}), bf16[16,2,6144]{2,1,0:T(2,128)(2,1)}, u32[]{:S(2)}, u32[]{:S(2)}) async-start(bf16[16,2,6144]{2,1,0:T(2,128)(2,1)} %reshape.787), calls=%async_computation.13 | async-start | bytes 786432 | tf_op jit(solution)/shard_map/all_to_all | solution.py:33
  539.9 11.2 %all-gather.13 = bf16[3,64,1024]{2,1,0:T(8,128)(2,1)S(1)} all-gather(bf16[3,64,256]{2,1,0:T(8,128)(2,1)S(1)} %get-tuple-element.91), channel_id=15, replica_groups=mesh['pole'=4,'row'=16,'col'=4] {'col'}, dimensions={2}, use_global_device_ids=true | all-gather | bytes 491520 | tf_op jit(solution)/shard_map/all_gather | solution.py:32
  560.3 9.1 %all-to-all-start.13 = ((bf16[16,2,6144]{2,1,0:T(2,128)(2,1)}), bf16[16,2,6144]{2,1,0:T(2,128)(2,1)S(1)}, u32[]{:S(2)}, u32[]{:S(2)}) async-start(bf16[16,2,6144]{2,1,0:T(2,128)(2,1)} %reshape.789), calls=%async_computation.14 | async-start | bytes 786432 | tf_op jit(solution)/shard_map/all_to_all | solution.py:33
  596.5 33.3 %reduce-scatter.5.cloned.1.call-done = f32[2,4,64,256]{3,2,1,0:T(8,128)} async-done(((f32[8,4,64,256]{3,2,1,0:T(8,128)}), f32[2,4,64,256]{3,2,1,0:T(8,128)}) %reduce-scatter.5.cloned.1.call-update) | async-done | bytes 524304 | tf_op jit(solution)/shard_map/reduce_scatter | solution.py:134
  (351 shorter events, 203.8 us)
Async XLA Ops:
  8.0 143.6 %all-gather.33.cloned.1.call-start = ((), (), s32[]{:S(2)}) async-start(), calls=%async_computation.20 | async-start | bytes 1114112 | tf_op jit(solution)/shard_map/all_gather | solution.py:27
  13.2 166.0 %all-gather.31.cloned.1.call-start = ((), (), s32[]{:S(2)}) async-start(), calls=%async_computation.19 | async-start | bytes 1114112 | tf_op jit(solution)/shard_map/all_gather | solution.py:27
  14.0 187.8 %all-gather.29.cloned.1.call-start = ((), (), s32[]{:S(2)}) async-start(), calls=%async_computation.18 | async-start | bytes 1114112 | tf_op jit(solution)/shard_map/all_gather | solution.py:27
  14.7 209.6 %all-gather.27.cloned.1.call-start = ((), (), s32[]{:S(2)}) async-start(), calls=%async_computation.17 | async-start | bytes 1114112 | tf_op jit(solution)/shard_map/all_gather | solution.py:27
  15.3 305.3 %all-gather.35.cloned.1.call-start = ((), (), s32[]{:S(2)}) async-start(), calls=%async_computation.22 | async-start | bytes 1671168 | tf_op jit(solution)/shard_map/all_gather | solution.py:27
  18.9 349.6 %all-gather.37.cloned.1.call-start = ((), (), s32[]{:S(2)}) async-start(), calls=%async_computation.23 | async-start | bytes 1671168 | tf_op jit(solution)/shard_map/all_gather | solution.py:27
  19.5 376.3 %all-gather.39.cloned.1.call-start = ((), (), s32[]{:S(2)}) async-start(), calls=%async_computation.24 | async-start | bytes 1671168 | tf_op jit(solution)/shard_map/all_gather | solution.py:27
  20.2 402.1 %all-gather.41.cloned.1.call-start = ((), (), s32[]{:S(2)}) async-start(), calls=%async_computation.25 | async-start | bytes 1671168 | tf_op jit(solution)/shard_map/all_gather | solution.py:27
  21.0 428.2 %all-gather.43.cloned.1.call-start = ((), (), s32[]{:S(2)}) async-start(), calls=%async_computation.26 | async-start | bytes 1671168 | tf_op jit(solution)/shard_map/all_gather | solution.py:27
  22.0 110.0 %copy-start.6 = (bf16[15,64,256]{2,1,0:T(8,128)(2,1)}, bf16[15,64,256]{2,1,0:T(8,128)(2,1)S(1)}, u32[]{:S(2)}) copy-start(bf16[15,64,256]{2,1,0:T(8,128)(2,1)S(1)} %fusion.239) | copy-start | bytes 1474564
  71.3 39.2 %all-to-all-start.1 = ((bf16[16,2,2048]{2,1,0:T(2,128)(2,1)}), bf16[16,2,2048]{2,1,0:T(2,128)(2,1)S(1)}, u32[]{:S(2)}, u32[]{:S(2)}) async-start(bf16[16,2,2048]{2,1,0:T(2,128)(2,1)} %reshape.763), calls=%async_computation.1 | async-start | bytes 262144 | tf_op jit(solution)/shard_map/all_to_all | solution.py:33
  110.5 19.6 %all-to-all-start = ((bf16[16,2,2048]{2,1,0:T(2,128)(2,1)}), bf16[16,2,2048]{2,1,0:T(2,128)(2,1)S(1)}, u32[]{:S(2)}, u32[]{:S(2)}) async-start(bf16[16,2,2048]{2,1,0:T(2,128)(2,1)} %reshape.765), calls=%async_computation | async-start | bytes 262144 | tf_op jit(solution)/shard_map/all_to_all | solution.py:33
  119.6 360.7 %all-gather.45.cloned.1.call-start = ((), (), s32[]{:S(2)}) async-start(), calls=%async_computation.27 | async-start | bytes 1671168 | tf_op jit(solution)/shard_map/all_gather | solution.py:27
  164.3 28.3 %all-to-all-start.5 = ((bf16[16,2,4096]{2,1,0:T(2,128)(2,1)}), bf16[16,2,4096]{2,1,0:T(2,128)(2,1)S(1)}, u32[]{:S(2)}, u32[]{:S(2)}) async-start(bf16[16,2,4096]{2,1,0:T(2,128)(2,1)} %reshape.767), calls=%async_computation.5 | async-start | bytes 524288 | tf_op jit(solution)/shard_map/all_to_all | solution.py:33
  192.6 22.8 %all-to-all-start.4 = ((bf16[16,2,4096]{2,1,0:T(2,128)(2,1)}), bf16[16,2,4096]{2,1,0:T(2,128)(2,1)}, u32[]{:S(2)}, u32[]{:S(2)}) async-start(bf16[16,2,4096]{2,1,0:T(2,128)(2,1)} %reshape.769), calls=%async_computation.4 | async-start | bytes 524288 | tf_op jit(solution)/shard_map/all_to_all | solution.py:33
  215.4 24.9 %all-to-all-start.3 = ((bf16[16,2,4096]{2,1,0:T(2,128)(2,1)}), bf16[16,2,4096]{2,1,0:T(2,128)(2,1)}, u32[]{:S(2)}, u32[]{:S(2)}) async-start(bf16[16,2,4096]{2,1,0:T(2,128)(2,1)} %reshape.771), calls=%async_computation.3 | async-start | bytes 524288 | tf_op jit(solution)/shard_map/all_to_all | solution.py:33
  226.5 25.6 %copy-start.24 = (bf16[16,2,4096]{2,1,0:T(2,128)(2,1)S(1)}, bf16[16,2,4096]{2,1,0:T(2,128)(2,1)}, u32[]{:S(2)}) copy-start(bf16[16,2,4096]{2,1,0:T(2,128)(2,1)} %copy-done.23) | copy-start | bytes 786436
  240.4 27.6 %all-to-all-start.2 = ((bf16[16,2,4096]{2,1,0:T(2,128)(2,1)}), bf16[16,2,4096]{2,1,0:T(2,128)(2,1)}, u32[]{:S(2)}, u32[]{:S(2)}) async-start(bf16[16,2,4096]{2,1,0:T(2,128)(2,1)} %reshape.773), calls=%async_computation.2 | async-start | bytes 524288 | tf_op jit(solution)/shard_map/all_to_all | solution.py:33
  249.3 257.1 %all-gather.47.cloned.1.call-start = ((), (), s32[]{:S(2)}) async-start(), calls=%async_computation.28 | async-start | bytes 1671168 | tf_op jit(solution)/shard_map/all_gather | solution.py:27
  273.6 22.8 %copy-start.26 = (bf16[1,2,1024,64]{2,3,1,0:T(8,128)(2,1)S(1)}, bf16[1,2,1024,64]{2,3,1,0:T(8,128)(2,1)}, u32[]{:S(2)}) copy-start(bf16[1,2,1024,64]{2,3,1,0:T(8,128)(2,1)} %all_to_all.188) | copy-start | bytes 786436
  345.9 38.4 %all-to-all-start.6 = ((bf16[16,2,6144]{2,1,0:T(2,128)(2,1)}), bf16[16,2,6144]{2,1,0:T(2,128)(2,1)S(1)}, u32[]{:S(2)}, u32[]{:S(2)}) async-start(bf16[16,2,6144]{2,1,0:T(2,128)(2,1)} %reshape.775), calls=%async_computation.7 | async-start | bytes 786432 | tf_op jit(solution)/shard_map/all_to_all | solution.py:33
  384.3 27.7 %all-to-all-start.7 = ((bf16[16,2,6144]{2,1,0:T(2,128)(2,1)}), bf16[16,2,6144]{2,1,0:T(2,128)(2,1)S(1)}, u32[]{:S(2)}, u32[]{:S(2)}) async-start(bf16[16,2,6144]{2,1,0:T(2,128)(2,1)} %reshape.777), calls=%async_computation.8 | async-start | bytes 786432 | tf_op jit(solution)/shard_map/all_to_all | solution.py:33
  393.6 143.5 %all-gather.49.cloned.1.call-start = ((), (), s32[]{:S(2)}) async-start(), calls=%async_computation.29 | async-start | bytes 1671168 | tf_op jit(solution)/shard_map/all_gather | solution.py:27
  412.0 26.6 %all-to-all-start.8 = ((bf16[16,2,6144]{2,1,0:T(2,128)(2,1)}), bf16[16,2,6144]{2,1,0:T(2,128)(2,1)S(1)}, u32[]{:S(2)}, u32[]{:S(2)}) async-start(bf16[16,2,6144]{2,1,0:T(2,128)(2,1)} %reshape.779), calls=%async_computation.9 | async-start | bytes 786432 | tf_op jit(solution)/shard_map/all_to_all | solution.py:33
  438.6 28.6 %all-to-all-start.9 = ((bf16[16,2,6144]{2,1,0:T(2,128)(2,1)}), bf16[16,2,6144]{2,1,0:T(2,128)(2,1)S(1)}, u32[]{:S(2)}, u32[]{:S(2)}) async-start(bf16[16,2,6144]{2,1,0:T(2,128)(2,1)} %reshape.781), calls=%async_computation.10 | async-start | bytes 786432 | tf_op jit(solution)/shard_map/all_to_all | solution.py:33
  467.1 29.6 %all-to-all-start.10 = ((bf16[16,2,6144]{2,1,0:T(2,128)(2,1)}), bf16[16,2,6144]{2,1,0:T(2,128)(2,1)}, u32[]{:S(2)}, u32[]{:S(2)}) async-start(bf16[16,2,6144]{2,1,0:T(2,128)(2,1)} %reshape.783), calls=%async_computation.11 | async-start | bytes 786432 | tf_op jit(solution)/shard_map/all_to_all | solution.py:33
  496.7 27.3 %all-to-all-start.11 = ((bf16[16,2,6144]{2,1,0:T(2,128)(2,1)}), bf16[16,2,6144]{2,1,0:T(2,128)(2,1)S(1)}, u32[]{:S(2)}, u32[]{:S(2)}) async-start(bf16[16,2,6144]{2,1,0:T(2,128)(2,1)} %reshape.785), calls=%async_computation.12 | async-start | bytes 786432 | tf_op jit(solution)/shard_map/all_to_all | solution.py:33
  505.5 91.0 %all-reduce.2.cloned.1.call-start = ((), (), s32[]{:S(2)}) async-start(), calls=%async_computation.16 | async-start | bytes 655360 | tf_op jit(solution)/shard_map/psum | solution.py:131
  524.0 36.3 %all-to-all-start.12 = ((bf16[16,2,6144]{2,1,0:T(2,128)(2,1)}), bf16[16,2,6144]{2,1,0:T(2,128)(2,1)}, u32[]{:S(2)}, u32[]{:S(2)}) async-start(bf16[16,2,6144]{2,1,0:T(2,128)(2,1)} %reshape.787), calls=%async_computation.13 | async-start | bytes 786432 | tf_op jit(solution)/shard_map/all_to_all | solution.py:33
  533.2 63.3 %reduce-scatter.3.cloned.1.call-start = ((), (), s32[]{:S(2)}) async-start(), calls=%async_computation.21 | async-start | bytes 983040 | tf_op jit(solution)/shard_map/reduce_scatter | solution.py:133
  560.3 27.8 %all-to-all-start.13 = ((bf16[16,2,6144]{2,1,0:T(2,128)(2,1)}), bf16[16,2,6144]{2,1,0:T(2,128)(2,1)S(1)}, u32[]{:S(2)}, u32[]{:S(2)}) async-start(bf16[16,2,6144]{2,1,0:T(2,128)(2,1)} %reshape.789), calls=%async_computation.14 | async-start | bytes 786432 | tf_op jit(solution)/shard_map/all_to_all | solution.py:33
  569.5 60.3 %reduce-scatter.5.cloned.1.call-start = ((), (), s32[]{:S(2)}) async-start(), calls=%async_computation.30 | async-start | bytes 2621440 | tf_op jit(solution)/shard_map/reduce_scatter | solution.py:134
  (53 other events, 554.9 us)
Sparse Core Ops, SparseCore 0:
  13.3 42.7 all-gather.32
  58.0 37.5 all-gather.30
  97.5 37.7 all-gather.28
  137.0 37.5 all-gather.26
  176.3 38.9 all-gather.34
  217.0 41.2 all-gather.36
  260.1 38.2 all-gather.38
  300.3 37.8 all-gather.40
  340.0 40.8 all-gather.42
  382.6 40.1 all-gather.44
  424.7 41.0 all-gather.46
  467.5 40.5 all-gather.48
Sparse Core Ops, SparseCore 1:
  508.9 46.0 all-reduce.1
  557.9 25.4 reduce-scatter.2
  596.5 33.2 reduce-scatter.4
where the time goes:
time: 651 us; the launch traced here: 639 us
  blocking collectives  271 us (42%)
  starting transfers between devices  142 us (22%)
  local copies, waits for them, and re-layouts  89.6 us (14%)
  between operations  40.8 us (6%)
  waiting for transfers between devices  39.9 us (6%)
  matrix products  39 us (6%)
  other arithmetic  17.2 us (3%)
    all_gather x14, blocking collectives, descend(): inverse_rows = lax.all_gather(inverse, 'col', axis=3, tiled=True)  160 us
    all_to_all x14, starting transfers between devices, descend(): lax.all_to_all(inverse_rows, 'row', split_axis=3, concat_axis=2, tiled=True)  141 us
    all_gather x7, blocking collectives, full_rows(): return lax.all_gather(blocks, 'col', axis=2, tiled=True)  67.8 us
    all_gather x2, blocking collectives, descend(): columns = lax.all_gather(factor, 'row', axis=2, tiled=True)  43.8 us
    unnamed x147, local copies, waits for them, and re-layouts  42.6 us
    reduce_scatter x1, waiting for transfers between devices, local(): lax.psum_scatter(three_sum, 'pole', scatter_dimension=0, tiled=True)  33.3 us
    dot_general x14, matrix products, descend(): jnp.einsum('xmik,xkj->xmij', panels, flat, preferred_element_type=jnp.flo...  28.4 us
    all_to_all x24, local copies, waits for them, and re-layouts, descend(): lax.all_to_all(inverse_rows, 'row', split_axis=3, concat_axis=2, tiled=True)  17.1 us
  transfers between devices with their start and end apart: 29, of which 1 were waited for; matrix products, arithmetic and copies ran while one was open for 20% of the time, Pallas kernels for 0%

commit v1 on v0

v1 whole, which is shorter than its diff:
```python
import jax
import jax.numpy as jnp
from jax import lax
from jax.experimental import pallas as pl
from jax.experimental.pallas import tpu as pltpu
from jax.sharding import PartitionSpec as P

MESH = pl.DeviceIdType.MESH
F32 = jnp.float32
BF16 = jnp.bfloat16
SUPB = 512
W = 1024
ROWS = 64
COLS = 256
ZN = 8
YN = 4
XN = 4

L2A, L2B, L1, D0, D1, D2, L3A, L3B, L3C = range(9)
TWO_AT = 32
ONE_AT = 44


def positions(parents_ref):
    two = [parents_ref[i] for i in range(4)]
    three = [parents_ref[4 + k] for k in range(8)]
    place_two = []
    for i in range(4):
        before = sum([(two[h] == two[i]).astype(jnp.int32) for h in range(i)], jnp.int32(0))
        place_two.append(2 * two[i] + before)
    place_three = []
    for k in range(8):
        before = sum([(three[h] == three[k]).astype(jnp.int32) for h in range(k)], jnp.int32(0))
        above = sum([jnp.where(three[k] == i, place_two[i], 0) for i in range(4)], jnp.int32(0))
        place_three.append(2 * above + before)
    return place_two, place_three


def node_at(places, place):
    return sum([jnp.where(p == place, i, 0) for i, p in enumerate(places)], jnp.int32(0))


def limits(sizes_ref):
    row = lax.axis_index("row") * ROWS
    col = lax.axis_index("col") * COLS
    row_sup, row_at = row // SUPB, row % SUPB
    col_sup, col_at = col // SUPB, col % SUPB
    return (lambda n: sizes_ref[n, row_sup] - row_at), (lambda n: sizes_ref[n, col_sup] - col_at)


def masked(block, rows_live, cols_live):
    rows = lax.broadcasted_iota(jnp.int32, (ROWS, COLS), 0) < rows_live
    cols = lax.broadcasted_iota(jnp.int32, (ROWS, COLS), 1) < cols_live
    return jnp.where(rows & cols, block.astype(F32), 0.0)


def prepare(one_ref, two_ref, three_ref, diag_ref, sizes_ref, parents_ref, keep_two_ref, keep_three_ref, out_ref):
    place_two, place_three = positions(parents_ref)
    rows_of, cols_of = limits(sizes_ref)
    for z in range(ZN):
        i, j = z // 4, z // 2
        n2 = node_at(place_two, j)
        n3 = node_at(place_three, z)
        c0, c1, c2, c3 = cols_of(0), cols_of(1 + i), cols_of(3 + n2), cols_of(7 + n3)
        r0, r1, r2 = rows_of(0), rows_of(1 + i), rows_of(3 + n2)
        out_ref[z, L2A] = masked(two_ref[n2, 0], r0 * keep_two_ref[n2], c2).astype(BF16)
        out_ref[z, L2B] = masked(two_ref[n2, 1], r1, c2).astype(BF16)
        out_ref[z, L1] = masked(one_ref[i], r0, c1).astype(BF16)
        out_ref[z, D0] = masked(diag_ref[0], r0, c0).astype(BF16)
        out_ref[z, D1] = masked(diag_ref[1 + i], r1, c1).astype(BF16)
        out_ref[z, D2] = masked(diag_ref[3 + n2], r2, c2).astype(BF16)
        out_ref[z, L3A] = masked(three_ref[n3, 0], r0 * keep_three_ref[n3, 0], c3).astype(BF16)
        out_ref[z, L3B] = masked(three_ref[n3, 1], r1 * keep_three_ref[n3, 1], c3).astype(BF16)
        out_ref[z, L3C] = masked(three_ref[n3, 2], r2, c3).astype(BF16)


def dot(a, b):
    return jnp.dot(a, b, preferred_element_type=F32)


def tree(
    in_ref,
    out_ref,
    mat,
    res,
    yab,
    ybb,
    za,
    zb,
    zc,
    yat,
    ybt,
    yct,
    z_send,
    z_recv,
    y_send,
    y_recv,
    f_send,
    f_recv,
    d_send,
    d_recv,
    o_send,
    o_recv,
    own_sem,
):
    row, y = lax.axis_index("row"), lax.axis_index("col")
    z, core = row // 2, row % 2
    other = row + 1 - 2 * core
    up, down = (y + 1) % YN, (y + YN - 1) % YN
    far = (y + 2) % YN

    barrier = pltpu.get_barrier_semaphore()
    for d in range(1, 16):
        pl.semaphore_signal(barrier, inc=1, device_id={"row": (row + d) % 16}, device_id_type=MESH)
    for peer in (up, down):
        pl.semaphore_signal(barrier, inc=1, device_id={"col": peer}, device_id_type=MESH)
    pl.semaphore_wait(barrier, 17)

    def cols(at, width=COLS):
        return pl.ds(pl.multiple_of(at * width, width), width)

    def remote(src, dst, send, recv, **device):
        return pltpu.make_async_remote_copy(
            src_ref=src, dst_ref=dst, send_sem=send, recv_sem=recv, device_id=device, device_id_type=MESH
        )

    def along_z(g, d):
        to = (z + d) % ZN
        blocks = pl.ds(3 * g, 3)
        return remote(
            in_ref.at[to, blocks],
            mat.at[blocks, z, core, :, cols(y)],
            z_send.at[g, d - 1],
            z_recv.at[g, d - 1],
            row=2 * to + core,
        )

    def along_y(b, way, to):
        piece = mat.at[b, :, core, :, cols(y)]
        return remote(piece, piece, y_send.at[b, way], y_recv.at[b, way], col=to)

    def onward(b, way, source, to):
        piece = mat.at[b, pl.ds(4 * way, 4), core, :, cols(source)]
        return remote(piece, piece, f_send.at[b, way], f_recv.at[b, way], col=to)

    def across(b, n, source):
        piece = mat.at[b, :, core, :, cols(source)]
        return remote(piece, piece, d_send.at[b, n], d_recv.at[b, n], row=other)

    own = pltpu.make_async_copy(in_ref.at[z], mat.at[:, z, core, :, cols(y)], own_sem)
    own.start()
    for g in range(3):
        for d in range(1, ZN):
            along_z(g, d).start()
    own.wait()

    def spread(b, carry):
        along_y(b, 0, up).start()
        along_y(b, 1, down).start()
        across(b, 0, y).start()
        return carry

    def forward(b, carry):
        along_y(b, 0, up).wait_recv()
        onward(b, 0, down, up).start()
        across(b, 1, down).start()
        along_y(b, 1, down).wait_recv()
        onward(b, 1, up, down).start()
        across(b, 2, up).start()
        return carry

    def finish(b, carry):
        onward(b, 0, down, up).wait_recv()
        onward(b, 1, up, down).wait_recv()
        across(b, 3, far).start()
        return carry

    for g in range(3):
        for d in range(1, ZN):
            along_z(g, d).wait_recv()
        lax.fori_loop(3 * g, 3 * g + 3, spread, 0)
    lax.fori_loop(0, 9, forward, 0)
    lax.fori_loop(0, 9, finish, 0)

    def settle(b, carry):
        along_y(b, 0, up).wait_send()
        along_y(b, 1, down).wait_send()
        onward(b, 0, down, up).wait_send()
        onward(b, 1, up, down).wait_send()
        for n, source in enumerate((y, down, up, far)):
            across(b, n, source).wait()
        return carry

    lax.fori_loop(0, 9, settle, 0)
    for g in range(3):
        for d in range(1, ZN):
            along_z(g, d).wait_send()

    mine = 2 * y + core
    half = 2 * y + z % 2

    def tall(b, t):
        return mat[b, pl.ds(2 * t, 2)].reshape(256, W)

    def wide(b, t):
        return mat[b, :, :, :, cols(t)].reshape(W, 256)

    def strip(b, at):
        return mat[b, :, :, :, cols(at, 128)].reshape(W, 128)

    def strip_at(b, t, at):
        return mat[b, pl.ds(2 * t, 2), :, :, cols(at, 128)].reshape(256, 128)

    def rows_at(t):
        return pl.ds(pl.multiple_of(t * 256, 256), 256)

    def first(t, carry):
        low = strip(L3C, mine)
        at = rows_at(t)
        yab[at, 0:128] = strip_at(L3A, t, mine).astype(F32) - dot(tall(L2A, t), low)
        yab[at, 128:256] = strip_at(L2A, t, half).astype(F32)
        ybb[at, 0:128] = (strip_at(L3B, t, mine).astype(F32) - dot(tall(L2B, t), low)).astype(BF16)
        ybb[at, 128:256] = strip_at(L2B, t, half)
        return carry

    lax.fori_loop(0, 4, first, 0)

    def second(t, carry):
        at = rows_at(t)
        top = yab[at, :] - dot(tall(L1, t), ybb[...])
        yat[0:256, at] = top.T.astype(BF16)
        yat[256:384, at] = strip_at(L1, t, half).astype(F32).T.astype(BF16)
        ybt[:, at] = ybb[at, :].astype(F32).T.astype(BF16)
        yct[:, at] = strip_at(L3C, t, mine).astype(F32).T.astype(BF16)
        return carry

    lax.fori_loop(0, 4, second, 0)

    def put(n, t, value):
        res[n, pl.ds(4 * t, 4)] = value.T.astype(BF16).reshape(4, ROWS, 128)

    def root_rows(t, carry):
        value = dot(yat[...], wide(D0, t))
        za[:, rows_at(t)] = value.astype(BF16)
        put(0, t, -value[0:128])
        put(4, t, -value[128:256])
        put(7, t, -value[256:384])
        return carry

    lax.fori_loop(0, 4, root_rows, 0)

    def one_rows(t, carry):
        back = dot(za[...], wide(L1, t))
        value = dot(ybt[...], wide(D1, t)) - back[0:256]
        zb[:, rows_at(t)] = value.astype(BF16)
        put(1, t, -value[0:128])
        put(5, t, -value[128:256])
        put(8, t, back[256:384])
        return carry

    lax.fori_loop(0, 4, one_rows, 0)

    def two_rows(t, carry):
        back = dot(za[0:256, :], wide(L2A, t)) + dot(zb[...], wide(L2B, t))
        value = dot(yct[...], wide(D2, t)) - back[0:128]
        zc[:, rows_at(t)] = value.astype(BF16)
        put(2, t, -value)
        put(6, t, back[128:256])
        return carry

    lax.fori_loop(0, 4, two_rows, 0)

    def three_rows(t, carry):
        value = dot(za[0:128, :], wide(L3A, t)) + dot(zb[0:128, :], wide(L3B, t)) + dot(zc[...], wide(L3C, t))
        put(3, t, value)
        return carry

    lax.fori_loop(0, 4, three_rows, 0)

    def three_to(d):
        to = (row + d) % 16
        return remote(
            res.at[0:4, to],
            out_ref.at[pl.ds(4 * z, 4), :, cols(core, 128)],
            o_send.at[d - 1],
            o_recv.at[d - 1],
            row=to,
        )

    def two_to(d):
        to = (z + d) % ZN
        return remote(
            res.at[4:7, 2 * to + core],
            out_ref.at[pl.ds(TWO_AT + 3 * (z // 2), 3), :, cols(z % 2, 128)],
            o_send.at[14 + d],
            o_recv.at[14 + d],
            row=2 * to + core,
        )

    def one_to(n, d):
        to = (z + ZN - d) % ZN
        return remote(
            res.at[7:9, 2 * to + core],
            out_ref.at[pl.ds(ONE_AT + 2 * (z // 4), 2), :, cols(z % 2, 128)],
            o_send.at[22 + n],
            o_recv.at[22 + n],
            row=2 * to + core,
        )

    def keep(blocks, at, count, side):
        here = pltpu.make_async_copy(
            res.at[blocks, row], out_ref.at[pl.ds(at, count), :, cols(side, 128)], own_sem
        )
        here.start()
        here.wait()

    for d in range(1, 16):
        three_to(d).start()
    for d in range(1, ZN):
        two_to(d).start()
    for n, d in enumerate((1, 4, 5)):
        one_to(n, d).start()
    keep(slice(0, 4), 4 * z, 4, core)
    keep(slice(4, 7), TWO_AT + 3 * (z // 2), 3, z % 2)
    keep(slice(7, 9), ONE_AT + 2 * (z // 4), 2, z % 2)
    for d in range(1, 16):
        three_to(d).wait()
    for d in range(1, ZN):
        two_to(d).wait()
    for n, d in enumerate((1, 4, 5)):
        one_to(n, d).wait()


def poles(
    blocks_ref,
    diag_ref,
    sizes_ref,
    parents_ref,
    weight_ref,
    top_ref,
    two_ref,
    three_ref,
    mine,
    theirs,
    top,
    tops,
    weights,
    own_weight,
    send,
    recv,
):
    pole = lax.axis_index("pole")
    barrier = pltpu.get_barrier_semaphore()
    for d in range(1, XN):
        pl.semaphore_signal(barrier, inc=1, device_id={"pole": (pole + d) % XN}, device_id_type=MESH)

    place_two, place_three = positions(parents_ref)
    rows_of, cols_of = limits(sizes_ref)

    def diagonal(n):
        return masked(diag_ref[n], rows_of(n), cols_of(n))

    own_weight[...] = jnp.full((8, 128), weight_ref[0], F32)
    top[0] = diagonal(0).astype(BF16)
    for i in range(2):
        top[1 + 2 * i] = blocks_ref[ONE_AT + 2 * i]
        top[2 + 2 * i] = (diagonal(1 + i) + blocks_ref[ONE_AT + 2 * i + 1].astype(F32)).astype(BF16)
    for i in range(4):
        at = TWO_AT + 3 * place_two[i]
        mine[i, 8] = blocks_ref[at]
        mine[i, 9] = blocks_ref[at + 1]
        mine[i, 10] = (diagonal(3 + i) + blocks_ref[at + 2].astype(F32)).astype(BF16)
    for k in range(8):
        at = 4 * place_three[k]
        to, first = k // 2, 4 * (k % 2)
        for q in range(3):
            mine[to, first + q] = blocks_ref[at + q]
        mine[to, first + 3] = (diagonal(7 + k) + blocks_ref[at + 3].astype(F32)).astype(BF16)

    def copies(d):
        to = (pole + d) % XN
        pairs = ((mine.at[to], theirs.at[d - 1]), (top, tops.at[d - 1]), (own_weight, weights.at[d - 1]))
        return [
            pltpu.make_async_remote_copy(
                src_ref=src,
                dst_ref=dst,
                send_sem=send.at[d - 1, n],
                recv_sem=recv.at[d - 1, n],
                device_id={"pole": to},
                device_id_type=MESH,
            )
            for n, (src, dst) in enumerate(pairs)
        ]

    pl.semaphore_wait(barrier, XN - 1)
    for d in range(1, XN):
        for copy in copies(d):
            copy.start()
    for d in range(1, XN):
        for copy in copies(d):
            copy.wait()

    scale = [weight_ref[0]] + [weights[d, 0:1, 0:1] for d in range(XN - 1)]

    def total(own, others):
        value = scale[0] * own.astype(F32)
        for d in range(XN - 1):
            value = value + scale[d + 1] * others(d).astype(F32)
        return value

    for n in range(5):
        top_ref[n] = total(top[n], lambda d: tops[d, n])
    for n in range(3):
        two_ref[0, n] = total(mine[pole, 8 + n], lambda d: theirs[d, 8 + n])
    for n in range(8):
        three_ref[n // 4, n % 4] = total(mine[pole, n], lambda d: theirs[d, n])


VMEM = pl.BlockSpec(memory_space=pltpu.VMEM)
SMEM = pl.BlockSpec(memory_space=pltpu.SMEM)
ANY = pl.BlockSpec(memory_space=pl.ANY)
GRANT = 52 * 1024 * 1024


def local(
    lower_one,
    lower_two,
    lower_three,
    diag_inverse,
    pole_weight,
    super_sizes,
    parents,
    keep_two,
    keep_three,
):
    one = lower_one.reshape(2, ROWS, COLS)
    two = lower_two.reshape(4, 2, ROWS, COLS)
    three = lower_three.reshape(8, 3, ROWS, COLS)
    diag = diag_inverse.reshape(15, ROWS, COLS)

    packed = pl.pallas_call(
        prepare,
        out_shape=jax.ShapeDtypeStruct((ZN, 9, ROWS, COLS), BF16),
        in_specs=[VMEM] * 4 + [SMEM] * 4,
        out_specs=VMEM,
        compiler_params=pltpu.CompilerParams(vmem_limit_bytes=GRANT),
    )(one, two, three, diag, super_sizes, parents, keep_two, keep_three)

    dma = pltpu.SemaphoreType.DMA
    blocks = pl.pallas_call(
        tree,
        out_shape=jax.ShapeDtypeStruct((48, ROWS, COLS), BF16),
        in_specs=[ANY],
        out_specs=ANY,
        scratch_shapes=[
            pltpu.VMEM((9, ZN, 2, ROWS, W), BF16),
            pltpu.VMEM((9, 16, ROWS, 128), BF16),
            pltpu.VMEM((W, 256), F32),
            pltpu.VMEM((W, 256), BF16),
            pltpu.VMEM((384, W), BF16),
            pltpu.VMEM((256, W), BF16),
            pltpu.VMEM((128, W), BF16),
            pltpu.VMEM((384, W), BF16),
            pltpu.VMEM((256, W), BF16),
            pltpu.VMEM((128, W), BF16),
            dma((3, 7)),
            dma((3, 7)),
            dma((9, 2)),
            dma((9, 2)),
            dma((9, 2)),
            dma((9, 2)),
            dma((9, 4)),
            dma((9, 4)),
            dma((25,)),
            dma((25,)),
            dma,
        ],
        compiler_params=pltpu.CompilerParams(
            collective_id=0, has_side_effects=True, vmem_limit_bytes=GRANT
        ),
    )(packed)

    return pl.pallas_call(
        poles,
        out_shape=(
            jax.ShapeDtypeStruct((5, ROWS, COLS), F32),
            jax.ShapeDtypeStruct((1, 3, ROWS, COLS), F32),
            jax.ShapeDtypeStruct((2, 4, ROWS, COLS), F32),
        ),
        in_specs=[VMEM, VMEM, SMEM, SMEM, SMEM],
        out_specs=(VMEM, VMEM, VMEM),
        scratch_shapes=[
            pltpu.VMEM((XN, 11, ROWS, COLS), BF16),
            pltpu.VMEM((XN - 1, 11, ROWS, COLS), BF16),
            pltpu.VMEM((5, ROWS, COLS), BF16),
            pltpu.VMEM((XN - 1, 5, ROWS, COLS), BF16),
            pltpu.VMEM((XN - 1, 8, 128), F32),
            pltpu.VMEM((8, 128), F32),
            dma((XN - 1, 3)),
            dma((XN - 1, 3)),
        ],
        compiler_params=pltpu.CompilerParams(
            collective_id=1, has_side_effects=True, vmem_limit_bytes=GRANT
        ),
    )(blocks, diag, super_sizes, parents, pole_weight)


def solution(mesh):
    placed = (
        P("pole", None, None, "row", "col"),
        P("pole", None, None, "row", "col"),
        P("pole", None, None, "row", "col"),
        P("pole", None, "row", "col"),
        P("pole"),
        P(),
        P(),
        P(),
        P(),
    )
    return jax.shard_map(
        local,
        mesh=mesh,
        in_specs=placed,
        out_specs=(
            P(None, "row", "col"),
            P("pole", None, "row", "col"),
            P("pole", None, "row", "col"),
        ),
        check_vma=False,
    )
```

time: 651 us -> 204 us (0.31); the launches traced: 639 us -> 201 us
  blocking collectives: 271 us -> 0 us
  Pallas kernels: 0 us -> 190 us
  starting transfers between devices: 142 us -> 0 us
  local copies, waits for them, and re-layouts: 89.6 us -> 10.1 us
  waiting for transfers between devices: 39.9 us -> 0 us
  between operations: 40.8 us -> 1.33 us
  matrix products: 39 us -> 0 us
  other arithmetic: 17.2 us -> 0 us
    all_gather x23 -> x0, blocking collectives: 271 us -> none  [the longest x14 160 us: descend(): inverse_rows = lax.all_gather(inverse, 'col', axis=3, tiled=True)]
    pallas_call x0 -> x3, Pallas kernels: none -> 190 us  [the longest x1 159 us: local(): pl.pallas_call(tree, out_shape=jax.ShapeDtypeStruct((48, ROWS, COLS), BF1...]
    all_to_all x14 -> x0, starting transfers between devices: 141 us -> none  [descend(): lax.all_to_all(inverse_rows, 'row', split_axis=3, concat_axis=2, tiled=True)]
    dot_general x28 -> x0, matrix products: 39 us -> none  [the longest x14 28.4 us: descend(): jnp.einsum('xmik,xkj->xmij', panels, flat, preferred_element_type=jnp.flo...]
    reduce_scatter x2 -> x0, waiting for transfers between devices: 33.3 us -> none  [the longest x1 33.3 us: local(): lax.psum_scatter(three_sum, 'pole', scatter_dimension=0, tiled=True)]
    unnamed x147 -> x23, local copies, waits for them, and re-layouts: 42.6 us -> 10.1 us
    all_to_all x24 -> x0, local copies, waits for them, and re-layouts: 17.1 us -> none  [descend(): lax.all_to_all(inverse_rows, 'row', split_axis=3, concat_axis=2, tiled=True)]
    another operation x16 -> x0, local copies, waits for them, and re-layouts: 13.4 us -> none
  transfers between devices with their start and end apart: 29 -> 0, of which waited for: 1 -> 0; matrix products, arithmetic and copies ran while one was open for 20% -> 0% of each run, Pallas kernels for 0% -> 0%
where the time goes in v1:
time: 204 us; the launch traced here: 201 us
  Pallas kernels  190 us (93%)
  local copies, waits for them, and re-layouts  10.1 us (5%)
    pallas_call x1, Pallas kernels, local(): pl.pallas_call(tree, out_shape=jax.ShapeDtypeStruct((48, ROWS, COLS), BF1...  159 us
    pallas_call x1, Pallas kernels, local(): pl.pallas_call(poles, out_shape=(jax.ShapeDtypeStruct((5, ROWS, COLS), F3...  28.1 us
    unnamed x23, local copies, waits for them, and re-layouts  10.1 us

profile of v1, /device:TPU:1, one launch (start us, length us, event | category | flops | bytes accessed | tf_op | source)
XLA Modules:
  0.0 201.4 jit_solution(15241936619645510346)
XLA Ops:
  0.6 0.8 copy.12.sizes_ref
  1.4 0.8 copy.13.keep_three_ref
  2.2 0.0 copy-start.1
  2.2 1.0 copy-done.1
  3.2 0.0 copy-start.3
  3.2 1.1 copy-done.3
  4.3 0.0 copy-start.4
  4.3 0.9 copy-done.4
  5.3 0.0 copy-start.5
  5.3 0.8 copy-done.5
  6.1 0.0 copy-start.6
  6.1 0.7 copy-done.6
  6.8 0.0 copy-start.8
  6.8 0.7 copy-done.8
  7.4 2.9 %shard_map.112.in_ref = bf16[8,9,64,256]{3,2,1,0:T(8,128)(2,1)} custom-call(bf16[2,64,256]{2,1,0:T(8,128)(2,1)S(1)} %bitcast.8, bf16[4,2,64,256]{3,2,1,0:T(8,128)(2,1)S(1)} %bitcast.7, bf16[8,3,64,256]{3,2,1,0:T(8,128)(2,1)S(1)} %bitcast.6, bf16[15,64,256]{2,1,0:T(8,128)(2,1)S(1)} %bitcast.4, s32[15,2]{1,0:T(8,128)S(1)} %copy.12.sizes_ref, s32[12]{0:T(128)S(1)} %copy-done.6, ...), custom_call_target="tpu_custom_call" | custom-call | tf_op jit(solution)/shard_map/pallas_call | solution.py:441
  10.3 0.0 copy-start.2
  10.3 0.0 copy-start.7
  10.3 159.0 %shard_map.113.blocks_ref = bf16[48,64,256]{2,1,0:T(8,128)(2,1)S(1)} custom-call(bf16[8,9,64,256]{3,2,1,0:T(8,128)(2,1)} %shard_map.112.in_ref), custom_call_target="tpu_custom_call" | custom-call | tf_op jit(solution)/shard_map/pallas_call | solution.py:450
  169.3 0.0 copy-start
  169.3 1.1 copy-done
  171.1 0.0 copy-done.2
  171.1 0.0 copy-done.7
  171.1 28.1 %shard_map.114 = (f32[5,64,256]{2,1,0:T(8,128)S(1)}, f32[1,3,64,256]{3,2,1,0:T(8,128)S(1)}, f32[2,4,64,256]{3,2,1,0:T(8,128)S(1)}) custom-call(bf16[48,64,256]{2,1,0:T(8,128)(2,1)} %copy-done, bf16[15,64,256]{2,1,0:T(8,128)(2,1)S(1)} %bitcast.5, s32[15,2]{1,0:T(8,128)S(1)} %copy.12.sizes_ref, s32[12]{0:T(128)S(1)} %copy-done.7, f32[1]{0:T(128)S(6)} %copy.18.weight_ref), custom_call_target="tpu_custom_call" | custom-call | tf_op jit(solution)/shard_map/pallas_call | solution.py:483
  199.2 0.7 copy.19
  199.9 0.7 copy.20
  200.6 0.8 copy.21
Async XLA Ops:
  2.2 1.0 copy-start.1
  3.2 1.1 copy-start.3
  4.3 0.9 copy-start.4
  5.3 0.8 copy-start.5
  6.1 0.7 copy-start.6
  6.8 0.7 copy-start.8
  10.3 160.8 %copy-start.2 = (bf16[1,15,64,256]{3,2,1,0:T(8,128)(2,1)S(1)}, bf16[1,15,64,256]{3,2,1,0:T(8,128)(2,1)}, u32[]{:S(2)}) copy-start(bf16[1,15,64,256]{3,2,1,0:T(8,128)(2,1)} %param.12) | copy-start | bytes 1474564
  10.3 160.8 %copy-start.7 = (s32[12]{0:T(128)S(1)}, s32[12]{0:T(128)}, u32[]{:S(2)}) copy-start(s32[12]{0:T(128)} %parents_ref.3) | copy-start | bytes 148
  169.3 1.1 copy-start

commit v2 on v1

v2 whole, which is shorter than its diff:
```python
import jax
import jax.numpy as jnp
from jax import lax
from jax.experimental import pallas as pl
from jax.experimental.pallas import tpu as pltpu
from jax.sharding import PartitionSpec as P

MESH = pl.DeviceIdType.MESH
F32 = jnp.float32
BF16 = jnp.bfloat16
SUPB = 512
W = 1024
ROWS = 64
COLS = 256
ZN = 8
YN = 4
XN = 4

L2A, L2B, L1, D0, D1, D2, L3A, L3B, L3C = range(9)


def positions(parents_ref):
    two = [parents_ref[i] for i in range(4)]
    three = [parents_ref[4 + k] for k in range(8)]
    place_two = []
    for i in range(4):
        before = sum([(two[h] == two[i]).astype(jnp.int32) for h in range(i)], jnp.int32(0))
        place_two.append(2 * two[i] + before)
    place_three = []
    for k in range(8):
        before = sum([(three[h] == three[k]).astype(jnp.int32) for h in range(k)], jnp.int32(0))
        above = sum([jnp.where(three[k] == i, place_two[i], 0) for i in range(4)], jnp.int32(0))
        place_three.append(2 * above + before)
    return place_two, place_three


def node_at(places, place):
    return sum([jnp.where(p == place, i, 0) for i, p in enumerate(places)], jnp.int32(0))


def limits(sizes_ref):
    row = lax.axis_index("row") * ROWS
    col = lax.axis_index("col") * COLS
    row_sup, row_at = row // SUPB, row % SUPB
    col_sup, col_at = col // SUPB, col % SUPB
    return (lambda n: sizes_ref[n, row_sup] - row_at), (lambda n: sizes_ref[n, col_sup] - col_at)


def masked(block, rows_live, cols_live):
    rows = lax.broadcasted_iota(jnp.int32, (ROWS, COLS), 0) < rows_live
    cols = lax.broadcasted_iota(jnp.int32, (ROWS, COLS), 1) < cols_live
    return jnp.where(rows & cols, block.astype(F32), 0.0)


def dot(a, b):
    return jnp.dot(a, b, preferred_element_type=F32)


BATCHES = (((0, 2), (4, 6), (7, 9)), ((2, 3), (6, 7), None), ((3, 4), None, None))


def tree(
    one_hbm,
    two_hbm,
    three_hbm,
    diag_hbm,
    sizes_ref,
    parents_ref,
    keep_two_ref,
    keep_three_ref,
    weight_ref,
    top_ref,
    out_two_ref,
    out_three_ref,
    one_ref,
    two_ref,
    three_ref,
    diag_ref,
    in_ref,
    mat,
    res,
    yab,
    ybb,
    za,
    zb,
    zc,
    yat,
    ybt,
    yct,
    got_a,
    got_b,
    got_c,
    mine_x,
    theirs,
    top,
    tops,
    weights,
    own_weight,
    load_sem,
    z_send,
    z_recv,
    y_send,
    y_recv,
    f_send,
    f_recv,
    d_send,
    d_recv,
    o_send,
    o_recv,
    keep_sem,
    x_send,
    x_recv,
    own_sem,
):
    pole, row, y = lax.axis_index("pole"), lax.axis_index("row"), lax.axis_index("col")
    z, core = row // 2, row % 2
    other = row + 1 - 2 * core
    up, down = (y + 1) % YN, (y + YN - 1) % YN
    far = (y + 2) % YN

    barrier = pltpu.get_barrier_semaphore()
    for d in range(1, 16):
        pl.semaphore_signal(barrier, inc=1, device_id={"row": (row + d) % 16}, device_id_type=MESH)
    for peer in (up, down):
        pl.semaphore_signal(barrier, inc=1, device_id={"col": peer}, device_id_type=MESH)
    for d in range(1, XN):
        pl.semaphore_signal(barrier, inc=1, device_id={"pole": (pole + d) % XN}, device_id_type=MESH)

    loads = [
        pltpu.make_async_copy(src, dst, load_sem.at[n])
        for n, (src, dst) in enumerate(
            ((two_hbm, two_ref), (one_hbm, one_ref), (diag_hbm, diag_ref), (three_hbm, three_ref))
        )
    ]
    for load in loads:
        load.start()

    place_two, place_three = positions(parents_ref)
    rows_of, cols_of = limits(sizes_ref)
    order_two = [node_at(place_two, j) for j in range(4)]
    order_three = [node_at(place_three, k) for k in range(8)]
    r0, c0 = rows_of(0), cols_of(0)
    r1, c1 = [rows_of(1 + i) for i in range(2)], [cols_of(1 + i) for i in range(2)]
    r2, c2 = [rows_of(3 + n) for n in order_two], [cols_of(3 + n) for n in order_two]
    c3 = [cols_of(7 + n) for n in order_three]
    load_of = {L2A: 0, L2B: 0, L1: 1, D0: 2, D1: 2, D2: 2, L3A: 3, L3B: 3, L3C: 3}

    def block(b, to):
        i, j = to // 4, to // 2
        n2, n3 = order_two[j], order_three[to]
        if b == L2A:
            return masked(two_ref[n2, 0], r0 * keep_two_ref[n2], c2[j])
        if b == L2B:
            return masked(two_ref[n2, 1], r1[i], c2[j])
        if b == L1:
            return masked(one_ref[i], r0, c1[i])
        if b == D0:
            return masked(diag_ref[0], r0, c0)
        if b == D1:
            return masked(diag_ref[1 + i], r1[i], c1[i])
        if b == D2:
            return masked(diag_ref[3 + n2], r2[j], c2[j])
        if b == L3A:
            return masked(three_ref[n3, 0], r0 * keep_three_ref[n3, 0], c3[to])
        if b == L3B:
            return masked(three_ref[n3, 1], r1[i] * keep_three_ref[n3, 1], c3[to])
        return masked(three_ref[n3, 2], r2[j], c3[to])

    def cols(at, width=COLS):
        return pl.ds(pl.multiple_of(at * width, width), width)

    def remote(src, dst, send, recv, **device):
        return pltpu.make_async_remote_copy(
            src_ref=src, dst_ref=dst, send_sem=send, recv_sem=recv, device_id=device, device_id_type=MESH
        )

    def along_z(b, d):
        to = (z + d) % ZN
        return remote(
            in_ref.at[to, b],
            mat.at[b, z, core, :, cols(y)],
            z_send.at[b, d - 1],
            z_recv.at[b, d - 1],
            row=2 * to + core,
        )

    def own_copy(b):
        return pltpu.make_async_copy(in_ref.at[z, b], mat.at[b, z, core, :, cols(y)], own_sem.at[b])

    def along_y(b, way, to):
        piece = mat.at[b, :, core, :, cols(y)]
        return remote(piece, piece, y_send.at[b, way], y_recv.at[b, way], col=to)

    def onward(b, way, source, to):
        piece = mat.at[b, pl.ds(4 * way, 4), core, :, cols(source)]
        return remote(piece, piece, f_send.at[b, way], f_recv.at[b, way], col=to)

    def across(b, n):
        piece = mat.at[b, :, core, :, cols((y, down, up, far)[n])]
        return remote(piece, piece, d_send.at[b, n], d_recv.at[b, n], row=other)

    loaded = set()

    def mask(b):
        if load_of[b] not in loaded:
            loaded.add(load_of[b])
            loads[load_of[b]].wait()
        for to in range(ZN):
            in_ref[to, b] = block(b, to).astype(BF16)

    def z_start(b):
        own_copy(b).start()
        for d in (4, 3, 5, 2, 6, 1, 7):
            along_z(b, d).start()

    def z_sent(b):
        for d in range(1, ZN):
            along_z(b, d).wait_send()

    def gathered(b):
        own_copy(b).wait()
        for d in range(1, ZN):
            along_z(b, d).wait_recv()
        across(b, 0).start()

    def spread(b):
        along_y(b, 0, up).start()
        along_y(b, 1, down).start()

    def forward(b):
        along_y(b, 0, up).wait_recv()
        onward(b, 0, down, up).start()
        along_y(b, 1, down).wait_recv()
        onward(b, 1, up, down).start()
        across(b, 1).start()
        across(b, 2).start()

    def finish(b):
        onward(b, 0, down, up).wait_recv()
        onward(b, 1, up, down).wait_recv()
        across(b, 3).start()

    def shared(b, first=0):
        for n in range(first, 4):
            across(b, n).wait_recv()

    mine = 2 * y + core
    half = 2 * y + z % 2

    def tall(b, t):
        return mat[b, pl.ds(2 * t, 2)].reshape(256, W)

    def wide(b, t):
        return mat[b, :, :, :, cols(t)].reshape(W, 256)

    def strip(b, at):
        return mat[b, :, :, :, cols(at, 128)].reshape(W, 128)

    def strip_at(b, t, at):
        return mat[b, pl.ds(2 * t, 2), :, :, cols(at, 128)].reshape(256, 128)

    def rows_at(t):
        return pl.ds(pl.multiple_of(t * 256, 256), 256)

    def first(t, carry):
        low = strip(L3C, mine)
        at = rows_at(t)
        yab[at, 0:128] = strip_at(L3A, t, mine).astype(F32) - dot(tall(L2A, t), low)
        yab[at, 128:256] = strip_at(L2A, t, half).astype(F32)
        ybb[at, 0:128] = (strip_at(L3B, t, mine).astype(F32) - dot(tall(L2B, t), low)).astype(BF16)
        ybb[at, 128:256] = strip_at(L2B, t, half)
        return carry

    def second(t, carry):
        at = rows_at(t)
        top = yab[at, :] - dot(tall(L1, t), ybb[...])
        yat[0:256, at] = top.T.astype(BF16)
        yat[256:384, at] = strip_at(L1, t, half).astype(F32).T.astype(BF16)
        ybt[:, at] = ybb[at, :].astype(F32).T.astype(BF16)
        yct[:, at] = strip_at(L3C, t, mine).astype(F32).T.astype(BF16)
        return carry

    def put(n, t, value):
        res[n, pl.ds(4 * t, 4)] = value.T.astype(BF16).reshape(4, ROWS, 128)

    def root_rows(t, carry):
        value = dot(yat[...], wide(D0, t))
        za[:, rows_at(t)] = value.astype(BF16)
        put(0, t, -value[0:128])
        put(4, t, -value[128:256])
        put(7, t, -value[256:384])
        return carry

    def one_rows(t, carry):
        back = dot(za[...], wide(L1, t))
        value = dot(ybt[...], wide(D1, t)) - back[0:256]
        zb[:, rows_at(t)] = value.astype(BF16)
        put(1, t, -value[0:128])
        put(5, t, -value[128:256])
        put(8, t, back[256:384])
        return carry

    def two_rows(t, carry):
        back = dot(za[0:256, :], wide(L2A, t)) + dot(zb[...], wide(L2B, t))
        value = dot(yct[...], wide(D2, t)) - back[0:128]
        zc[:, rows_at(t)] = value.astype(BF16)
        put(2, t, -value)
        put(6, t, back[128:256])
        return carry

    def three_rows(t, carry):
        value = dot(za[0:128, :], wide(L3A, t)) + dot(zb[0:128, :], wide(L3B, t)) + dot(zc[...], wide(L3C, t))
        put(3, t, value)
        return carry

    gots = (got_a, got_b, got_c)
    one_offsets = (1, 4, 5)

    def batch_copies(n):
        got = gots[n]
        three, two, one = BATCHES[n]
        count = three[1] - three[0]
        copies = []
        for d in range(1, 16):
            to = (row + d) % 16
            copies.append((res.at[three[0] : three[1], to], got.at[pl.ds(z * count, count), :, cols(core, 128)], to))
        if two is not None:
            at = ZN * count + (z // 2) * count
            for d in range(1, ZN):
                to = 2 * ((z + d) % ZN) + core
                copies.append((res.at[two[0] : two[1], to], got.at[pl.ds(at, count), :, cols(z % 2, 128)], to))
        if one is not None:
            at = (ZN + 4) * count + (z // 4) * count
            for d in one_offsets:
                to = 2 * ((z + ZN - d) % ZN) + core
                copies.append((res.at[one[0] : one[1], to], got.at[pl.ds(at, count), :, cols(z % 2, 128)], to))
        return [
            remote(src, dst, o_send.at[n, k], o_recv.at[n, k], row=to) for k, (src, dst, to) in enumerate(copies)
        ]

    def batch_kept(n):
        got = gots[n]
        three, two, one = BATCHES[n]
        count = three[1] - three[0]
        copies = [(three, z * count, core)]
        if two is not None:
            copies.append((two, (ZN + z // 2) * count, z % 2))
        if one is not None:
            copies.append((one, (ZN + 4 + z // 4) * count, z % 2))
        return [
            pltpu.make_async_copy(
                res.at[blocks[0] : blocks[1], row],
                got.at[pl.ds(at, count), :, cols(side, 128)],
                keep_sem.at[n, k],
            )
            for k, (blocks, at, side) in enumerate(copies)
        ]

    def leave(n):
        for copy in batch_copies(n) + batch_kept(n):
            copy.start()

    def landed(n):
        for copy in batch_kept(n):
            copy.wait()
        for copy in batch_copies(n):
            copy.wait_recv()

    def diagonal(n):
        return masked(diag_ref[n], rows_of(n), cols_of(n))

    X_BATCHES = ((0, 6), (6, 9), (9, 11))

    def pole_copies(n):
        copies = []
        for d in range(1, XN):
            to = (pole + d) % XN
            blocks = slice(*X_BATCHES[n])
            pairs = [(mine_x.at[to, blocks], theirs.at[d - 1, blocks])]
            if n == 0:
                pairs += [(top, tops.at[d - 1]), (own_weight, weights.at[d - 1])]
            for k, (src, dst) in enumerate(pairs):
                copies.append(remote(src, dst, x_send.at[n, d - 1, k], x_recv.at[n, d - 1, k], pole=to))
        return copies

    def order_a():
        own_weight[...] = jnp.full((8, 128), weight_ref[0], F32)
        top[0] = diagonal(0).astype(BF16)
        for i in range(2):
            top[1 + 2 * i] = got_a[24 + 2 * i]
            top[2 + 2 * i] = (diagonal(1 + i) + got_a[25 + 2 * i].astype(F32)).astype(BF16)
        for i in range(4):
            mine_x[i, 4] = got_a[16 + 2 * place_two[i]]
            mine_x[i, 5] = got_a[17 + 2 * place_two[i]]
        for k in range(8):
            at = 2 * (k % 2)
            mine_x[k // 2, at] = got_a[2 * place_three[k]]
            mine_x[k // 2, at + 1] = got_a[2 * place_three[k] + 1]

    def order_b():
        for i in range(4):
            mine_x[i, 8] = (diagonal(3 + i) + got_b[8 + place_two[i]].astype(F32)).astype(BF16)
        for k in range(8):
            mine_x[k // 2, 6 + k % 2] = got_b[place_three[k]]

    def order_c():
        for k in range(8):
            mine_x[k // 2, 9 + k % 2] = (diagonal(7 + k) + got_c[place_three[k]].astype(F32)).astype(BF16)

    def to_poles(n):
        for copy in pole_copies(n):
            copy.start()

    def from_poles(n):
        for copy in pole_copies(n):
            copy.wait_recv()

    def total(own, others):
        value = weight_ref[0] * own.astype(F32)
        for d in range(XN - 1):
            value = value + weights[d, 0:1, 0:1] * others(d).astype(F32)
        return value

    def summed(n):
        return total(mine_x[pole, n], lambda d: theirs[d, n])

    def stage(body):
        lax.fori_loop(0, 4, body, 0)

    mask(0)
    pl.semaphore_wait(barrier, 15 + 2 + 3)
    z_start(0)
    for b in range(1, 9):
        mask(b)
    z_sent(0)
    z_start(1)
    gathered(0)
    spread(0)
    z_sent(1)
    z_start(2)
    gathered(1)
    spread(1)
    z_sent(2)
    z_start(3)
    gathered(2)
    forward(0)
    spread(2)
    z_sent(3)
    z_start(4)
    gathered(3)
    forward(1)
    spread(3)
    finish(0)
    z_sent(4)
    z_start(5)
    gathered(4)
    z_sent(5)
    z_start(6)
    forward(2)
    spread(4)
    finish(1)
    gathered(5)
    z_sent(6)
    z_start(7)
    gathered(6)
    forward(3)
    spread(5)
    finish(2)
    z_sent(7)
    z_start(8)
    gathered(7)
    shared(0)
    shared(1)
    forward(4)
    spread(6)
    finish(3)
    gathered(8)
    for b in (6, 7, 8):
        across(b, 0).wait_recv()
    stage(first)
    shared(2)
    stage(second)
    forward(5)
    spread(7)
    finish(4)
    shared(3)
    stage(root_rows)
    shared(4)
    stage(one_rows)
    leave(0)
    forward(6)
    spread(8)
    finish(5)
    shared(5)
    stage(two_rows)
    leave(1)
    forward(7)
    finish(6)
    landed(0)
    order_a()
    to_poles(0)
    forward(8)
    finish(7)
    landed(1)
    order_b()
    to_poles(1)
    finish(8)
    for b in (6, 7, 8):
        shared(b, 1)
    stage(three_rows)
    leave(2)
    from_poles(0)
    for n in range(5):
        top_ref[n] = total(top[n], lambda d: tops[d, n])
    for n in range(2):
        out_two_ref[0, n] = summed(4 + n)
    for n in range(4):
        out_three_ref[n // 2, n % 2] = summed(n)
    landed(2)
    order_c()
    to_poles(2)
    from_poles(1)
    out_two_ref[0, 2] = summed(8)
    for n in range(2):
        out_three_ref[n, 2] = summed(6 + n)
    from_poles(2)
    for n in range(2):
        out_three_ref[n, 3] = summed(9 + n)

    z_sent(8)
    for b in range(9):
        along_y(b, 0, up).wait_send()
        along_y(b, 1, down).wait_send()
        onward(b, 0, down, up).wait_send()
        onward(b, 1, up, down).wait_send()
        for n in range(4):
            across(b, n).wait_send()
    for n in range(3):
        for copy in batch_copies(n) + pole_copies(n):
            copy.wait_send()


VMEM = pl.BlockSpec(memory_space=pltpu.VMEM)
SMEM = pl.BlockSpec(memory_space=pltpu.SMEM)
ANY = pl.BlockSpec(memory_space=pl.ANY)
GRANT = 52 * 1024 * 1024


def local(
    lower_one,
    lower_two,
    lower_three,
    diag_inverse,
    pole_weight,
    super_sizes,
    parents,
    keep_two,
    keep_three,
):
    one = lower_one.reshape(2, ROWS, COLS)
    two = lower_two.reshape(4, 2, ROWS, COLS)
    three = lower_three.reshape(8, 3, ROWS, COLS)
    diag = diag_inverse.reshape(15, ROWS, COLS)

    dma = pltpu.SemaphoreType.DMA
    return pl.pallas_call(
        tree,
        out_shape=(
            jax.ShapeDtypeStruct((5, ROWS, COLS), F32),
            jax.ShapeDtypeStruct((1, 3, ROWS, COLS), F32),
            jax.ShapeDtypeStruct((2, 4, ROWS, COLS), F32),
        ),
        in_specs=[ANY] * 4 + [SMEM] * 5,
        out_specs=(VMEM, VMEM, VMEM),
        scratch_shapes=[
            pltpu.VMEM((2, ROWS, COLS), BF16),
            pltpu.VMEM((4, 2, ROWS, COLS), BF16),
            pltpu.VMEM((8, 3, ROWS, COLS), BF16),
            pltpu.VMEM((15, ROWS, COLS), BF16),
            pltpu.VMEM((ZN, 9, ROWS, COLS), BF16),
            pltpu.VMEM((9, ZN, 2, ROWS, W), BF16),
            pltpu.VMEM((9, 16, ROWS, 128), BF16),
            pltpu.VMEM((W, 256), F32),
            pltpu.VMEM((W, 256), BF16),
            pltpu.VMEM((384, W), BF16),
            pltpu.VMEM((256, W), BF16),
            pltpu.VMEM((128, W), BF16),
            pltpu.VMEM((384, W), BF16),
            pltpu.VMEM((256, W), BF16),
            pltpu.VMEM((128, W), BF16),
            pltpu.VMEM((28, ROWS, COLS), BF16),
            pltpu.VMEM((12, ROWS, COLS), BF16),
            pltpu.VMEM((8, ROWS, COLS), BF16),
            pltpu.VMEM((XN, 11, ROWS, COLS), BF16),
            pltpu.VMEM((XN - 1, 11, ROWS, COLS), BF16),
            pltpu.VMEM((5, ROWS, COLS), BF16),
            pltpu.VMEM((XN - 1, 5, ROWS, COLS), BF16),
            pltpu.VMEM((XN - 1, 8, 128), F32),
            pltpu.VMEM((8, 128), F32),
            dma((4,)),
            dma((9, 7)),
            dma((9, 7)),
            dma((9, 2)),
            dma((9, 2)),
            dma((9, 2)),
            dma((9, 2)),
            dma((9, 4)),
            dma((9, 4)),
            dma((3, 25)),
            dma((3, 25)),
            dma((3, 3)),
            dma((3, XN - 1, 3)),
            dma((3, XN - 1, 3)),
            dma((9,)),
        ],
        compiler_params=pltpu.CompilerParams(
            collective_id=0, has_side_effects=True, vmem_limit_bytes=GRANT
        ),
    )(one, two, three, diag, super_sizes, parents, keep_two, keep_three, pole_weight)


def solution(mesh):
    placed = (
        P("pole", None, None, "row", "col"),
        P("pole", None, None, "row", "col"),
        P("pole", None, None, "row", "col"),
        P("pole", None, "row", "col"),
        P("pole"),
        P(),
        P(),
        P(),
        P(),
    )
    return jax.shard_map(
        local,
        mesh=mesh,
        in_specs=placed,
        out_specs=(
            P(None, "row", "col"),
            P("pole", None, "row", "col"),
            P("pole", None, "row", "col"),
        ),
        check_vma=False,
    )
```

time: 204 us -> 138 us (0.68); the launches traced: 201 us -> 138 us
  Pallas kernels: 190 us -> 129 us
  local copies, waits for them, and re-layouts: 10.1 us -> 7.03 us
    pallas_call x3 -> x1, Pallas kernels: 190 us -> 129 us  [local(): pl.pallas_call(tree, out_shape=(jax.ShapeDtypeStruct((5, ROWS, COLS), F32...]
    unnamed x23 -> x19, local copies, waits for them, and re-layouts: 10.1 us -> 7.03 us
where the time goes in v2:
time: 138 us
  Pallas kernels  129 us (93%)
  local copies, waits for them, and re-layouts  7.03 us (5%)
    pallas_call x1, Pallas kernels, local(): pl.pallas_call(tree, out_shape=(jax.ShapeDtypeStruct((5, ROWS, COLS), F32...  129 us
    unnamed x19, local copies, waits for them, and re-layouts  7.03 us

profile of v2, /device:TPU:1, one launch (start us, length us, event | category | flops | bytes accessed | tf_op | source)
XLA Modules:
  0.0 137.7 jit_solution(10095439773447599004)
XLA Ops:
  1.3 0.0 copy-start.5
  1.3 0.7 copy-done.5
  2.0 0.0 copy-start.6
  2.0 0.1 copy.13.keep_three_ref
  2.0 0.6 copy-done.6
  2.6 0.0 copy-start.3
  2.6 0.0 copy-start.4
  2.6 0.1 copy.12.sizes_ref
  2.7 0.6 copy-done.3
  3.3 0.0 copy-done.4
  3.3 0.0 copy-start
  3.3 1.0 copy-done
  4.3 0.0 copy-start.1
  4.3 0.9 copy-done.1
  5.3 0.0 copy-start.2
  5.3 0.8 copy-done.2
  6.1 129.3 %shard_map.112 = (f32[5,64,256]{2,1,0:T(8,128)S(1)}, f32[1,3,64,256]{3,2,1,0:T(8,128)S(1)}, f32[2,4,64,256]{3,2,1,0:T(8,128)S(1)}) custom-call(bf16[2,64,256]{2,1,0:T(8,128)(2,1)S(1)} %bitcast.6, bf16[4,2,64,256]{3,2,1,0:T(8,128)(2,1)S(1)} %bitcast.5, bf16[8,3,64,256]{3,2,1,0:T(8,128)(2,1)} %bitcast.7, bf16[15,64,256]{2,1,0:T(8,128)(2,1)S(1)} %bitcast.4, ...), custom_call_target="tpu_custom_call" | custom-call | tf_op jit(solution)/shard_map/pallas_call | solution.py:566
  135.5 0.7 copy.18
  136.2 0.7 copy.19
  136.9 0.8 copy.20
Async XLA Ops:
  1.3 0.7 copy-start.5
  2.0 0.7 copy-start.6
  2.6 0.7 copy-start.3
  2.6 0.7 copy-start.4
  3.3 1.0 copy-start
  4.3 0.9 copy-start.1
  5.3 0.8 copy-start.2

commit v3 on v2

v3 whole, which is shorter than its diff:
```python
import jax
import jax.numpy as jnp
from jax import lax
from jax.experimental import pallas as pl
from jax.experimental.pallas import tpu as pltpu
from jax.sharding import PartitionSpec as P

MESH = pl.DeviceIdType.MESH
F32 = jnp.float32
BF16 = jnp.bfloat16
SUPB = 512
W = 1024
ROWS = 64
COLS = 256
ZN = 8
YN = 4
XN = 4

L2A, L2B, L1, D0, D1, D2, L3A, L3B, L3C = range(9)


def mod(a, n):
    return a % n if isinstance(a, int) else lax.rem(a, n)


def div(a, n):
    return a // n if isinstance(a, int) else lax.div(a, n)


def positions(parents_ref):
    two = [parents_ref[i] for i in range(4)]
    three = [parents_ref[4 + k] for k in range(8)]
    place_two = []
    for i in range(4):
        before = sum([(two[h] == two[i]).astype(jnp.int32) for h in range(i)], jnp.int32(0))
        place_two.append(2 * two[i] + before)
    place_three = []
    for k in range(8):
        before = sum([(three[h] == three[k]).astype(jnp.int32) for h in range(k)], jnp.int32(0))
        above = sum([jnp.where(three[k] == i, place_two[i], 0) for i in range(4)], jnp.int32(0))
        place_three.append(2 * above + before)
    return place_two, place_three


def node_at(places, place):
    return sum([jnp.where(p == place, i, 0) for i, p in enumerate(places)], jnp.int32(0))


def limits(sizes_ref):
    row = lax.axis_index("row") * ROWS
    col = lax.axis_index("col") * COLS
    row_sup, row_at = div(row, SUPB), mod(row, SUPB)
    col_sup, col_at = div(col, SUPB), mod(col, SUPB)
    return (lambda n: sizes_ref[row_sup, n] - row_at), (lambda n: sizes_ref[col_sup, n] - col_at)


def below(limit, axis):
    places = lax.broadcasted_iota(jnp.int32, (ROWS, COLS), axis)
    return jnp.where(places < limit, 1.0, 0.0).astype(BF16)


def dot(a, b):
    return jnp.dot(a, b, preferred_element_type=F32)


X3A, X2A, X1, X3B, X2B, P1, X3C, P2, P3 = range(9)
BATCHES = 4
SHARE = {L2A: 2, L2B: 2, L1: 4, D0: 8, D1: 4, D2: 2, L3A: 1, L3B: 1, L3C: 1}
PART = ROWS // XN


def tree(
    one_hbm,
    two_hbm,
    three_hbm,
    diag_hbm,
    sizes_ref,
    parents_ref,
    keep_two_ref,
    keep_three_ref,
    weight_ref,
    top_ref,
    out_two_ref,
    out_three_ref,
    one_ref,
    two_ref,
    three_ref,
    diag_ref,
    in_ref,
    mat,
    res,
    yab,
    ybb,
    za,
    zb,
    zc,
    yat,
    ybt,
    yct,
    got_a,
    got_b,
    got_c,
    got_d,
    terms,
    sums,
    diag_mine,
    diag_theirs,
    diag_sum,
    mine_two,
    mine_three,
    mine_top,
    weights,
    own_weight,
    load_sem,
    z_send,
    z_recv,
    y_send,
    y_recv,
    f_recv,
    d_send,
    d_recv,
    s_recv,
    o_send,
    o_recv,
    x_send,
    x_recv,
    p_send,
    p_recv,
    g_send,
    g_recv,
):
    pole, row, y = lax.axis_index("pole"), lax.axis_index("row"), lax.axis_index("col")
    z, core = div(row, 2), mod(row, 2)
    other = row + 1 - 2 * core
    up, down = mod((y + 1), YN), mod((y + YN - 1), YN)
    far = mod((y + 2), YN)

    loads = [
        pltpu.make_async_copy(src, dst, load_sem.at[n])
        for n, (src, dst) in enumerate(
            ((two_hbm, two_ref), (one_hbm, one_ref), (diag_hbm, diag_ref), (three_hbm, three_ref))
        )
    ]
    for load in loads:
        load.start()

    barrier = pltpu.get_barrier_semaphore()
    for d in range(1, 16):
        pl.semaphore_signal(barrier, inc=1, device_id={"row": mod((row + d), 16)}, device_id_type=MESH)
    for peer in (up, down):
        pl.semaphore_signal(barrier, inc=1, device_id={"col": peer}, device_id_type=MESH)
    for d in range(1, XN):
        pl.semaphore_signal(barrier, inc=1, device_id={"pole": mod((pole + d), XN)}, device_id_type=MESH)

    place_two, place_three = positions(parents_ref)
    rows_of, cols_of = limits(sizes_ref)
    order_two = [node_at(place_two, j) for j in range(4)]
    order_three = [node_at(place_three, k) for k in range(8)]
    r0, c0 = rows_of(0), cols_of(0)
    r1, c1 = [rows_of(1 + i) for i in range(2)], [cols_of(1 + i) for i in range(2)]
    r2, c2 = [rows_of(3 + n) for n in order_two], [cols_of(3 + n) for n in order_two]
    c3 = [cols_of(7 + n) for n in order_three]
    load_of = {L2A: 0, L2B: 0, L1: 1, D0: 2, D1: 2, D2: 2, L3A: 3, L3B: 3, L3C: 3}

    def block(b, to):
        i, j = div(to, 4), div(to, 2)
        n2, n3 = order_two[j], order_three[to]
        if b == L2A:
            return two_ref[n2, 0] * rows[0] * below(c2[j] * keep_two_ref[n2], 1)
        if b == L2B:
            return two_ref[n2, 1] * rows[1 + i] * below(c2[j], 1)
        if b == L1:
            return one_ref[i] * rows[0] * below(c1[i], 1)
        if b == D0:
            return diag_ref[0] * rows[0] * below(c0, 1)
        if b == D1:
            return diag_ref[1 + i] * rows[1 + i] * below(c1[i], 1)
        if b == D2:
            return diag_ref[3 + n2] * rows[3 + j] * below(c2[j], 1)
        if b == L3A:
            return three_ref[n3, 0] * rows[0] * below(c3[to] * keep_three_ref[0, n3], 1)
        if b == L3B:
            return three_ref[n3, 1] * rows[1 + i] * below(c3[to] * keep_three_ref[1, n3], 1)
        return three_ref[n3, 2] * rows[3 + j] * below(c3[to], 1)

    rows, loaded = {}, set()

    def mask(b):
        if load_of[b] not in loaded:
            loaded.add(load_of[b])
            loads[load_of[b]].wait()
        for n in {L2B: (1, 2), D1: (1, 2), D2: (3, 4, 5, 6), L3B: (1, 2), L3C: (3, 4, 5, 6)}.get(b, (0,)):
            if n not in rows:
                rows[n] = below(r0 if n == 0 else r1[n - 1] if n < 3 else r2[n - 3], 0)
        for to in range(0, ZN, SHARE[b]):
            in_ref[to, b] = block(b, to)

    def cols(at, width=COLS):
        return pl.ds(pl.multiple_of(at * width, width), width)

    def remote(src, dst, send, recv, **device):
        return pltpu.make_async_remote_copy(
            src_ref=src, dst_ref=dst, send_sem=send, recv_sem=recv, device_id=device, device_id_type=MESH
        )

    def along_z(b, d):
        to = mod((z + d), ZN)
        return remote(
            in_ref.at[div(to, SHARE[b]) * SHARE[b], b],
            mat.at[b, z, core, :, cols(y)],
            z_send.at[b],
            z_recv.at[b],
            row=2 * to + core,
        )

    def own_copy(b):
        return pltpu.make_async_copy(
            in_ref.at[div(z, SHARE[b]) * SHARE[b], b], mat.at[b, z, core, :, cols(y)], z_recv.at[b]
        )

    def along_y(b, way, to):
        piece = mat.at[b, :, core, :, cols(y)]
        return remote(piece, piece, y_send.at[b], y_recv.at[b, way], col=to)

    def onward(b, way, source, to):
        piece = mat.at[b, pl.ds(4 * way, 4), core, :, cols(source)]
        return remote(piece, piece, y_send.at[b], f_recv.at[b, way], col=to)

    def across(b, n):
        piece = mat.at[b, :, core, :, cols((y, down, up, far)[n])]
        return remote(piece, piece, d_send.at[b], d_recv.at[b, min(n, 1)], row=other)

    def z_start(b):
        own_copy(b).start()
        for d in (4, 3, 5, 2, 6, 1, 7):
            along_z(b, d).start()

    def arrived(ref, sem):
        pltpu.make_async_copy(ref, ref, sem).wait()

    def z_sent(b):
        arrived(mat.at[b, 0 : ZN - 1, core, :, cols(y)], z_send.at[b])

    def gathered(b):
        arrived(mat.at[b, :, core, :, cols(y)], z_recv.at[b])
        across(b, 0).start()

    PIECES = ((1, 1), (2, 1), (3, 3), (2, 3), (1, 3), (2, 2))

    def piece_at(b, i, j):
        return mat.at[b, pl.ds(2 * (mod((y + YN + i), YN)), 2), core, :, cols(mod((y + YN + j), YN))]

    def piece_copy(b, n):
        i, j = PIECES[n]
        if n < 2:
            piece, to = piece_at(b, i - 1, j - 1), down
        elif n < 5:
            piece, to = piece_at(b, i - 3, j - 3), up
        else:
            piece, to = piece_at(b, 1, 1), down
        return remote(piece, piece, y_send.at[b], s_recv.at[b - D0, (0, 1, 1, 1, 1, 2)[n]], col=to)

    def piece_across(b, n):
        piece = piece_at(b, *PIECES[n])
        return remote(piece, piece, d_send.at[b], d_recv.at[b, 1], row=other)

    def spread(b):
        if D0 <= b <= D2:
            for n in (0, 2, 1, 3, 4):
                piece_copy(b, n).start()
            return
        along_y(b, 0, up).start()
        along_y(b, 1, down).start()

    def forward(b):
        if D0 <= b <= D2:
            piece_copy(b, 0).wait_recv()
            piece_copy(b, 5).start()
            arrived(mat.at[b, 0:4, core, :, 0 : 2 * COLS], s_recv.at[b - D0, 1])
            for n in range(5):
                piece_across(b, n).start()
            return
        along_y(b, 0, up).wait_recv()
        onward(b, 0, down, up).start()
        along_y(b, 1, down).wait_recv()
        onward(b, 1, up, down).start()
        across(b, 1).start()
        across(b, 2).start()

    def finish(b):
        if D0 <= b <= D2:
            piece_copy(b, 5).wait_recv()
            piece_across(b, 5).start()
            return
        onward(b, 0, down, up).wait_recv()
        onward(b, 1, up, down).wait_recv()
        across(b, 3).start()

    def strip_shared(b):
        across(b, 0).wait_recv()

    def shared(b):
        if b not in (L3A, L3B, L3C):
            strip_shared(b)
        if D0 <= b <= D2:
            arrived(mat.at[b, 0:6, core, :, 0 : 2 * COLS], d_recv.at[b, 1])
        else:
            arrived(mat.at[b, :, core, :, 0 : 3 * COLS], d_recv.at[b, 1])

    def settle(b):
        if D0 <= b <= D2:
            arrived(mat.at[b, 0:6, core, :, 0 : 2 * COLS], y_send.at[b])
            arrived(mat.at[b, 0:5, core], d_send.at[b])
        else:
            arrived(mat.at[b, 0:6, core], y_send.at[b])
            arrived(mat.at[b, :, core], d_send.at[b])

    mine = 2 * y + core
    half = 2 * y + mod(z, 2)

    def tall(b, t):
        return mat[b, pl.ds(2 * t, 2)].reshape(256, W)

    def wide(b, t):
        return mat[b, :, :, :, cols(t)].reshape(W, 256)

    def strip(b, at):
        return mat[b, :, :, :, cols(at, 128)].reshape(W, 128)

    def strip_at(b, t, at):
        return mat[b, pl.ds(2 * t, 2), :, :, cols(at, 128)].reshape(256, 128)

    def rows_at(t):
        return pl.ds(pl.multiple_of(t * 256, 256), 256)

    def first(t, carry):
        low = strip(L3C, mine)
        at = rows_at(t)
        yab[at, 0:128] = strip_at(L3A, t, mine).astype(F32) - dot(tall(L2A, t), low)
        yab[at, 128:256] = strip_at(L2A, t, half).astype(F32)
        ybb[at, 0:128] = (strip_at(L3B, t, mine).astype(F32) - dot(tall(L2B, t), low)).astype(BF16)
        ybb[at, 128:256] = strip_at(L2B, t, half)
        return carry

    def second(t, carry):
        at = rows_at(t)
        top = yab[at, :] - dot(tall(L1, t), ybb[...])
        yat[0:256, at] = top.T.astype(BF16)
        yat[256:384, at] = strip_at(L1, t, half).astype(F32).T.astype(BF16)
        ybt[:, at] = ybb[at, :].astype(F32).T.astype(BF16)
        yct[:, at] = strip_at(L3C, t, mine).astype(F32).T.astype(BF16)
        return carry

    def put(n, t, value):
        parts = value.T.astype(BF16).reshape(2, 2, XN, PART, 128)
        for q in range(XN):
            for side in range(2):
                res[n, q, side, div(t, 2), mod(t, 2)] = parts[:, side, q]

    def symmetric(left, b, j):
        value = None
        for i in range(YN):
            at = rows_at(mod((y + i), YN))
            if j == 0 or (i, j) in PIECES:
                piece = mat[b, pl.ds(2 * (mod((y + i), YN)), 2), :, :, cols(mod((y + j), YN))].reshape(COLS, COLS)
                term = dot(left[:, at], piece)
            else:
                piece = mat[b, pl.ds(2 * (mod((y + j), YN)), 2), :, :, cols(mod((y + i), YN))].reshape(COLS, COLS)
                term = lax.dot_general(left[:, at], piece, (((1,), (1,)), ((), ())), preferred_element_type=F32)
            value = term if value is None else value + term
        return value

    def root_rows():
        for j in range(YN):
            t = mod((y + j), YN)
            value = symmetric(yat, D0, j)
            za[:, rows_at(t)] = value.astype(BF16)
            put(X3A, t, -value[0:128])
            put(X2A, t, -value[128:256])
            put(X1, t, -value[256:384])

    def one_rows():
        for j in range(YN):
            t = mod((y + j), YN)
            back = dot(za[...], wide(L1, t))
            value = symmetric(ybt, D1, j) - back[0:256]
            zb[:, rows_at(t)] = value.astype(BF16)
            put(X3B, t, -value[0:128])
            put(X2B, t, -value[128:256])
            put(P1, t, back[256:384])

    def two_rows():
        for j in range(YN):
            t = mod((y + j), YN)
            back = dot(za[0:256, :], wide(L2A, t)) + dot(zb[...], wide(L2B, t))
            value = symmetric(yct, D2, j) - back[0:128]
            zc[:, rows_at(t)] = value.astype(BF16)
            put(X3C, t, -value)
            put(P2, t, back[128:256])

    def three_rows(t, carry):
        value = dot(za[0:128, :], wide(L3A, t)) + dot(zb[0:128, :], wide(L3B, t)) + dot(zc[...], wide(L3C, t))
        put(P3, t, value)
        return carry

    gots = (got_a, got_b, got_c, got_d)
    fork = mod((div(z, 2)), 2)

    def batch(n):
        two, one = (core,), (core, slice(None), fork)
        return (
            ((X3A, ()), (X2A, two), (X1, one)),
            ((X3B, ()), (X2B, two), (P1, one)),
            ((X3C, ()), (P2, two)),
            ((P3, ()),),
        )[n]

    def term_copies(n):
        copies = []
        for d in range(1, XN):
            to = mod((pole + d), XN)
            for k, (b, place) in enumerate(batch(n)):
                copies.append(
                    remote(
                        res.at[(b, to) + place],
                        terms.at[(d - 1, b) + place],
                        x_send.at[n, d - 1, k],
                        x_recv.at[n, d - 1, k],
                        pole=to,
                    )
                )
        return copies

    def diag_copies():
        copies = []
        for d in range(1, XN):
            to = mod((pole + d), XN)
            pairs = ((diag_mine.at[:, to], diag_theirs.at[d - 1]), (own_weight, weights.at[d - 1]))
            for k, (src, dst) in enumerate(pairs):
                copies.append(remote(src, dst, p_send.at[d - 1, k], p_recv.at[d - 1, k], pole=to))
        return copies

    def weighted(own, others):
        value = weight_ref[0] * own.astype(F32)
        for d in range(XN - 1):
            value = value + weights[d, 0:1, 0:1] * others(d).astype(F32)
        return value

    def start(copies):
        for copy in copies:
            copy.start()

    def received(copies):
        for copy in copies:
            copy.wait_recv()

    def mask_diagonals():
        own_weight[...] = jnp.full((8, 128), weight_ref[0], F32)
        for n in range(15):
            live = below(rows_of(n), 0) * below(cols_of(n), 1)
            diag_mine[n] = (diag_ref[n] * live).reshape(XN, PART, COLS)

    def sum_diagonals():
        received(diag_copies())
        for n in range(15):
            diag_sum[n] = weighted(diag_mine[n, pole], lambda d: diag_theirs[d, n])

    def sum_terms(n):
        received(term_copies(n))
        for b, place in batch(n):
            at = (b,) + place
            sums[at] = weighted(res[(b, pole) + place], lambda d: terms[(d,) + at])

    def batch_copies(n):
        got = gots[n]
        levels = batch(n)
        copies = []
        for d in range(1, 16):
            to = mod((row + d), 16)
            to_z, side = div(to, 2), mod(to, 2)
            src = sums.at[levels[0][0], side, div(to_z, 4), mod((div(to_z, 2)), 2), mod(to_z, 2)]
            copies.append((src, got.at[z, :, cols(core, 128)], to))
        if len(levels) > 1:
            for d in range(1, ZN):
                to_z = mod((z + d), ZN)
                src = sums.at[levels[1][0], core, div(to_z, 4), mod((div(to_z, 2)), 2), mod(to_z, 2)]
                copies.append((src, got.at[ZN + div(z, 2), :, cols(mod(z, 2), 128)], 2 * to_z + core))
        if len(levels) > 2:
            for dh, dp in ((0, 1), (1, 0), (1, 1)):
                h, p = mod((div(z, 4) + dh), 2), mod((z + dp), 2)
                to_z = 4 * h + 2 * fork + p
                src = sums.at[levels[2][0], core, h, fork, p]
                copies.append((src, got.at[ZN + 4 + div(z, 4), :, cols(mod(z, 2), 128)], 2 * to_z + core))
        return [
            remote(src, dst, o_send.at[n], o_recv.at[n], row=to) for src, dst, to in copies
        ]

    def batch_kept(n):
        places = ((z, core), (ZN + div(z, 2), mod(z, 2)), (ZN + 4 + div(z, 4), mod(z, 2)))
        return [
            pltpu.make_async_copy(
                sums.at[b, core, div(z, 4), fork, mod(z, 2)], gots[n].at[at, :, cols(side, 128)], o_recv.at[n]
            )
            for (b, _), (at, side) in zip(batch(n), places)
        ]

    def leave(n):
        start(batch_copies(n) + batch_kept(n))

    def landed(n):
        arrived(gots[n], o_recv.at[n])

    def order(n):
        got = gots[n]
        if n == 0:
            mine_top[0] = diag_sum[0]
        for i in range(2):
            if n == 0:
                mine_top[1 + 2 * i] = got[12 + i]
            elif n == 1:
                mine_top[2 + 2 * i] = diag_sum[1 + i] + got[12 + i]
        for i in range(4):
            if n < 3:
                value = got[8 + place_two[i]]
                mine_two[i, n] = value + diag_sum[3 + i] if n == 2 else value
        for k in range(8):
            value = got[place_three[k]]
            mine_three[div(k, 2), mod(k, 2), n] = value + diag_sum[7 + k] if n == 3 else value

    part = pl.ds(pl.multiple_of(pole * PART, PART), PART)

    def owner_copies(n):
        copies = []
        for d in range(1, XN):
            to = mod((pole + d), XN)
            pairs = [(mine_three.at[to, :, n], out_three_ref.at[:, n, part])]
            if n < 3:
                pairs.append((mine_two.at[to, n], out_two_ref.at[0, n, part]))
            if n == 1:
                pairs.append((mine_top, top_ref.at[:, part]))
            for k, (src, dst) in enumerate(pairs):
                copies.append(remote(src, dst, g_send.at[n, d - 1, k], g_recv.at[n, d - 1, k], pole=to))
        return copies

    def to_owner(n):
        landed(n)
        order(n)
        start(owner_copies(n))
        for k in range(2):
            out_three_ref[k, n, part] = mine_three[pole, k, n]
        if n < 3:
            out_two_ref[0, n, part] = mine_two[pole, n]
        if n == 1:
            for b in range(5):
                top_ref[b, part] = mine_top[b]

    def stage(body):
        lax.fori_loop(0, 4, body, 0)

    mask(L2A)
    pl.semaphore_wait(barrier, 15 + 2 + 3)
    z_start(L2A)
    mask(L2B)
    mask(L1)
    z_sent(L2A)
    z_start(L2B)
    z_start(L1)
    mask(D0)
    mask(L3C)
    gathered(L2A)
    spread(L2A)
    mask(L3B)
    mask(L3A)
    z_sent(L2B)
    z_start(D0)
    gathered(L2B)
    spread(L2B)
    mask(D1)
    mask(D2)
    z_sent(L1)
    z_start(L3C)
    forward(L2A)
    gathered(L1)
    spread(L1)
    mask_diagonals()
    start(diag_copies())
    z_sent(D0)
    z_start(L3B)
    forward(L2B)
    finish(L2A)
    gathered(D0)
    spread(D0)
    z_sent(L3C)
    z_start(L3A)
    forward(L1)
    finish(L2B)
    gathered(L3C)
    spread(L3C)
    z_sent(L3B)
    z_start(D1)
    forward(D0)
    finish(L1)
    gathered(L3B)
    spread(L3B)
    sum_diagonals()
    z_sent(L3A)
    z_start(D2)
    gathered(L3A)
    shared(L2A)
    shared(L2B)
    for b in (L3A, L3B, L3C):
        strip_shared(b)
    stage(first)
    forward(L3C)
    finish(D0)
    z_sent(D1)
    gathered(D1)
    spread(D1)
    shared(L1)
    stage(second)
    z_sent(D2)
    gathered(D2)
    spread(D2)
    spread(L3A)
    shared(D0)
    root_rows()
    start(term_copies(0))
    forward(L3B)
    finish(L3C)
    forward(D1)
    finish(D1)
    shared(D1)
    one_rows()
    start(term_copies(1))
    forward(D2)
    finish(L3B)
    finish(D2)
    sum_terms(0)
    leave(0)
    shared(D2)
    two_rows()
    start(term_copies(2))
    forward(L3A)
    sum_terms(1)
    leave(1)
    finish(L3A)
    for b in (L3A, L3B, L3C):
        shared(b)
    stage(three_rows)
    start(term_copies(3))
    to_owner(0)
    sum_terms(2)
    leave(2)
    sum_terms(3)
    leave(3)
    to_owner(1)
    to_owner(2)
    to_owner(3)
    for n in range(BATCHES):
        received(owner_copies(n))

    for b in range(9):
        settle(b)
    for n in range(BATCHES):
        if n == 2:
            arrived(got_b.at[0:11], o_send.at[n])
        else:
            arrived(mat.at[0 : (5, 5, 0, 3)[n], 0:5, 0, 0:32, 0:128], o_send.at[n])
        for copy in term_copies(n) + owner_copies(n):
            copy.wait_send()
    for copy in diag_copies():
        copy.wait_send()


VMEM = pl.BlockSpec(memory_space=pltpu.VMEM)
SMEM = pl.BlockSpec(memory_space=pltpu.SMEM)
HBM = pl.BlockSpec(memory_space=pltpu.HBM)
GRANT = 58 * 1024 * 1024


def local(
    lower_one,
    lower_two,
    lower_three,
    diag_inverse,
    pole_weight,
    super_sizes,
    parents,
    keep_two,
    keep_three,
):
    one = lower_one.reshape(2, ROWS, COLS)
    two = lower_two.reshape(4, 2, ROWS, COLS)
    three = lower_three.reshape(8, 3, ROWS, COLS)
    diag = diag_inverse.reshape(15, ROWS, COLS)

    dma = pltpu.SemaphoreType.DMA
    return pl.pallas_call(
        tree,
        out_shape=(
            jax.ShapeDtypeStruct((5, ROWS, COLS), F32),
            jax.ShapeDtypeStruct((1, 3, ROWS, COLS), F32),
            jax.ShapeDtypeStruct((2, 4, ROWS, COLS), F32),
        ),
        in_specs=[HBM] * 4 + [SMEM] * 5,
        out_specs=(VMEM, VMEM, VMEM),
        scratch_shapes=[
            pltpu.VMEM((2, ROWS, COLS), BF16),
            pltpu.VMEM((4, 2, ROWS, COLS), BF16),
            pltpu.VMEM((8, 3, ROWS, COLS), BF16),
            pltpu.VMEM((15, ROWS, COLS), BF16),
            pltpu.VMEM((ZN, 9, ROWS, COLS), BF16),
            pltpu.VMEM((9, ZN, 2, ROWS, W), BF16),
            pltpu.VMEM((9, XN, 2, 2, 2, 2, PART, 128), BF16),
            pltpu.VMEM((W, 256), F32),
            pltpu.VMEM((W, 256), BF16),
            pltpu.VMEM((384, W), BF16),
            pltpu.VMEM((256, W), BF16),
            pltpu.VMEM((128, W), BF16),
            pltpu.VMEM((384, W), BF16),
            pltpu.VMEM((256, W), BF16),
            pltpu.VMEM((128, W), BF16),
            pltpu.VMEM((14, PART, COLS), F32),
            pltpu.VMEM((14, PART, COLS), F32),
            pltpu.VMEM((12, PART, COLS), F32),
            pltpu.VMEM((8, PART, COLS), F32),
            pltpu.VMEM((XN - 1, 9, 2, 2, 2, 2, PART, 128), BF16),
            pltpu.VMEM((9, 2, 2, 2, 2, PART, 128), F32),
            pltpu.VMEM((15, XN, PART, COLS), BF16),
            pltpu.VMEM((XN - 1, 15, PART, COLS), BF16),
            pltpu.VMEM((15, PART, COLS), F32),
            pltpu.VMEM((XN, 3, PART, COLS), F32),
            pltpu.VMEM((XN, 2, 4, PART, COLS), F32),
            pltpu.VMEM((5, PART, COLS), F32),
            pltpu.VMEM((XN - 1, 8, 128), F32),
            pltpu.VMEM((8, 128), F32),
            dma((4,)),
            dma((9,)),
            dma((9,)),
            dma((9,)),
            dma((9, 2)),
            dma((9, 2)),
            dma((9,)),
            dma((9, 2)),
            dma((3, 3)),
            dma((BATCHES,)),
            dma((BATCHES,)),
            dma((BATCHES, XN - 1, 3)),
            dma((BATCHES, XN - 1, 3)),
            dma((XN - 1, 2)),
            dma((XN - 1, 2)),
            dma((BATCHES, XN - 1, 3)),
            dma((BATCHES, XN - 1, 3)),
        ],
        compiler_params=pltpu.CompilerParams(
            collective_id=0, has_side_effects=True, vmem_limit_bytes=GRANT
        ),
    )(one, two, three, diag, super_sizes.T, parents, keep_two, keep_three.T, pole_weight)


def solution(mesh):
    placed = (
        P("pole", None, None, "row", "col"),
        P("pole", None, None, "row", "col"),
        P("pole", None, None, "row", "col"),
        P("pole", None, "row", "col"),
        P("pole"),
        P(),
        P(),
        P(),
        P(),
    )
    return jax.shard_map(
        local,
        mesh=mesh,
        in_specs=placed,
        out_specs=(
            P(None, "row", "col"),
            P("pole", None, "row", "col"),
            P("pole", None, "row", "col"),
        ),
        check_vma=False,
    )
```

time: 138 us -> 123 us (0.89)
  Pallas kernels: 129 us -> 117 us
  local copies, waits for them, and re-layouts: 7.03 us -> 4.19 us
    pallas_call x1, Pallas kernels: 129 us -> 117 us  [local(): pl.pallas_call(tree, out_shape=(jax.ShapeDtypeStruct((5, ROWS, COLS), F32...]
    unnamed x19 -> x5, local copies, waits for them, and re-layouts: 7.03 us -> 4.19 us
where the time goes in v3:
time: 123 us
  Pallas kernels  117 us (95%)
  local copies, waits for them, and re-layouts  4.19 us (3%)
  between operations  1.3 us (1%)
    pallas_call x1, Pallas kernels, local(): pl.pallas_call(tree, out_shape=(jax.ShapeDtypeStruct((5, ROWS, COLS), F32...  117 us
    unnamed x5, local copies, waits for them, and re-layouts  4.19 us

profile of v3, /device:TPU:1, one launch (start us, length us, event | category | flops | bytes accessed | tf_op | source)
XLA Modules:
  0.0 122.5 jit_solution(4460171153145447908)
XLA Ops:
  1.3 117.0 %shard_map.112 = (f32[5,64,256]{2,1,0:T(8,128)}, f32[1,3,64,256]{3,2,1,0:T(8,128)}, f32[2,4,64,256]{3,2,1,0:T(8,128)}) custom-call(bf16[2,64,256]{2,1,0:T(8,128)(2,1)} %bitcast.9, bf16[4,2,64,256]{3,2,1,0:T(8,128)(2,1)} %bitcast.8, bf16[8,3,64,256]{3,2,1,0:T(8,128)(2,1)} %bitcast.6, bf16[15,64,256]{2,1,0:T(8,128)(2,1)} %bitcast.7, s32[2,15]{1,0:T(2,128)} %bitcast.10, ...), custom_call_target="tpu_custom_call" | custom-call | tf_op jit(solution)/shard_map/pallas_call | solution.py:698
  118.3 0.0 copy-start
  118.3 1.8 %copy.16 = f32[5,64,256]{2,1,0:T(8,128)} copy(f32[5,64,256]{2,1,0:T(8,128)} %get-tuple-element.6) | data formatting | bytes 655360
  120.1 1.6 %copy.17 = f32[1,3,64,256]{3,2,1,0:T(8,128)} copy(f32[1,3,64,256]{3,2,1,0:T(8,128)} %get-tuple-element.7) | data formatting | bytes 393216
  121.7 0.0 copy-done
  121.7 0.8 copy.18
Async XLA Ops:
  118.3 3.4 %copy-start = (f32[2,4,64,256]{3,2,1,0:T(8,128)S(1)}, f32[2,4,64,256]{3,2,1,0:T(8,128)}, u32[]{:S(2)}) copy-start(f32[2,4,64,256]{3,2,1,0:T(8,128)} %get-tuple-element.8) | copy-start | bytes 1572868

commit v4 on v3

--- a/solution.py
+++ b/solution.py
@@ -94,6 +94,7 @@
     za,
     zb,
     zc,
+    acc,
     yat,
     ybt,
     yct,
@@ -109,6 +110,9 @@
     mine_two,
     mine_three,
     mine_top,
+    full_two,
+    full_three,
+    full_top,
     weights,
     own_weight,
     load_sem,
@@ -228,7 +232,7 @@
 
     def across(b, n):
         piece = mat.at[b, :, core, :, cols((y, down, up, far)[n])]
-        return remote(piece, piece, d_send.at[b], d_recv.at[b, min(n, 1)], row=other)
+        return remote(piece, piece, d_send.at[b], d_recv.at[b, (0, 1, 1, 2)[n]], row=other)
 
     def z_start(b):
         own_copy(b).start()
@@ -299,13 +303,17 @@
     def strip_shared(b):
         across(b, 0).wait_recv()
 
+    def neighbours_shared(b):
+        arrived(mat.at[b, :, core, :, 0 : 2 * COLS], d_recv.at[b, 1])
+
     def shared(b):
         if b not in (L3A, L3B, L3C):
             strip_shared(b)
         if D0 <= b <= D2:
             arrived(mat.at[b, 0:6, core, :, 0 : 2 * COLS], d_recv.at[b, 1])
         else:
-            arrived(mat.at[b, :, core, :, 0 : 3 * COLS], d_recv.at[b, 1])
+            neighbours_shared(b)
+            across(b, 3).wait_recv()
 
     def settle(b):
         if D0 <= b <= D2:
@@ -398,10 +406,13 @@
             put(X3C, t, -value)
             put(P2, t, back[128:256])
 
-    def three_rows(t, carry):
-        value = dot(za[0:128, :], wide(L3A, t)) + dot(zb[0:128, :], wide(L3B, t)) + dot(zc[...], wide(L3C, t))
-        put(P3, t, value)
+    def three_begin(t, carry):
+        acc[:, rows_at(t)] = dot(zb[0:128, :], wide(L3B, t)) + dot(zc[...], wide(L3C, t))
         return carry
+
+    def three_rows(j):
+        t = mod(y + j, YN)
+        put(P3, t, acc[:, rows_at(t)] + dot(za[0:128, :], wide(L3A, t)))
 
     gots = (got_a, got_b, got_c, got_d)
     fork = mod((div(z, 2)), 2)
@@ -412,7 +423,6 @@
             ((X3A, ()), (X2A, two), (X1, one)),
             ((X3B, ()), (X2B, two), (P1, one)),
             ((X3C, ()), (P2, two)),
-            ((P3, ()),),
         )[n]
 
     def term_copies(n):
@@ -469,7 +479,41 @@
         received(term_copies(n))
         for b, place in batch(n):
             at = (b,) + place
-            sums[at] = weighted(res[(b, pole) + place], lambda d: terms[(d,) + at])
+            sums[at] = weighted(res[(b, pole) + place], lambda d: terms[(d,) + at]).astype(BF16)
+
+    def quarter_place(j):
+        t = mod(y + j, YN)
+        return (slice(None), div(t, 2), mod(t, 2))
+
+    def quarter_copies(j):
+        place = quarter_place(j)
+        copies = []
+        for d in range(1, XN):
+            src, dst = (P3, mod(pole + d, XN)) + place, (d - 1, P3) + place
+            copies.append(
+                remote(
+                    res.at[src], terms.at[dst], x_send.at[3, d - 1, j], x_recv.at[3, d - 1, j], pole=mod(pole + d, XN)
+                )
+            )
+        return copies
+
+    def leave_quarter(j):
+        received(quarter_copies(j))
+        place = quarter_place(j)
+        sums[(P3,) + place] = weighted(res[(P3, pole) + place], lambda d: terms[(d, P3) + place]).astype(BF16)
+        for p in range(2):
+            for side in range(2):
+                to = 4 * mod(y + j, YN) + 2 * p + side
+                src = sums.at[P3, side, place[1], place[2], p]
+                dst = got_d.at[z, :, cols(core, 128)]
+
+                @pl.when(to != row)
+                def _():
+                    remote(src, dst, o_send.at[3], o_recv.at[3], row=to).start()
+
+                @pl.when(to == row)
+                def _():
+                    pltpu.make_async_copy(src, dst, o_recv.at[3]).start()
 
     def batch_copies(n):
         got = gots[n]
@@ -512,32 +556,34 @@
 
     def order(n):
         got = gots[n]
+
+        def with_diagonal(value, node):
+            return (value.astype(F32) + diag_sum[node]).astype(BF16)
+
         if n == 0:
-            mine_top[0] = diag_sum[0]
+            mine_top[0] = diag_sum[0].astype(BF16)
         for i in range(2):
             if n == 0:
                 mine_top[1 + 2 * i] = got[12 + i]
             elif n == 1:
-                mine_top[2 + 2 * i] = diag_sum[1 + i] + got[12 + i]
+                mine_top[2 + 2 * i] = with_diagonal(got[12 + i], 1 + i)
         for i in range(4):
             if n < 3:
                 value = got[8 + place_two[i]]
-                mine_two[i, n] = value + diag_sum[3 + i] if n == 2 else value
+                mine_two[i, n] = with_diagonal(value, 3 + i) if n == 2 else value
         for k in range(8):
             value = got[place_three[k]]
-            mine_three[div(k, 2), mod(k, 2), n] = value + diag_sum[7 + k] if n == 3 else value
-
-    part = pl.ds(pl.multiple_of(pole * PART, PART), PART)
+            mine_three[k // 2, k % 2, n] = with_diagonal(value, 7 + k) if n == 3 else value
 
     def owner_copies(n):
         copies = []
         for d in range(1, XN):
             to = mod((pole + d), XN)
-            pairs = [(mine_three.at[to, :, n], out_three_ref.at[:, n, part])]
+            pairs = [(mine_three.at[to, :, n], full_three.at[pole, :, n])]
             if n < 3:
-                pairs.append((mine_two.at[to, n], out_two_ref.at[0, n, part]))
+                pairs.append((mine_two.at[to, n], full_two.at[pole, n]))
             if n == 1:
-                pairs.append((mine_top, top_ref.at[:, part]))
+                pairs.append((mine_top, full_top.at[pole]))
             for k, (src, dst) in enumerate(pairs):
                 copies.append(remote(src, dst, g_send.at[n, d - 1, k], g_recv.at[n, d - 1, k], pole=to))
         return copies
@@ -546,13 +592,23 @@
         landed(n)
         order(n)
         start(owner_copies(n))
-        for k in range(2):
-            out_three_ref[k, n, part] = mine_three[pole, k, n]
+        full_three[pole, :, n] = mine_three[pole, :, n]
         if n < 3:
-            out_two_ref[0, n, part] = mine_two[pole, n]
+            full_two[pole, n] = mine_two[pole, n]
         if n == 1:
-            for b in range(5):
-                top_ref[b, part] = mine_top[b]
+            full_top[pole] = mine_top[...]
+
+    def write(n):
+        received(owner_copies(n))
+        for q in range(XN):
+            part = slice(q * PART, (q + 1) * PART)
+            for k in range(2):
+                out_three_ref[k, n, part] = full_three[q, k, n].astype(F32)
+            if n < 3:
+                out_two_ref[0, n, part] = full_two[q, n].astype(F32)
+            if n == 1:
+                for b in range(5):
+                    top_ref[b, part] = full_top[q, b].astype(F32)
 
     def stage(body):
         lax.fori_loop(0, 4, body, 0)
@@ -627,6 +683,8 @@
     start(term_copies(0))
     forward(L3B)
     finish(L3C)
+    sum_terms(0)
+    leave(0)
     forward(D1)
     finish(D1)
     shared(D1)
@@ -635,29 +693,34 @@
     forward(D2)
     finish(L3B)
     finish(D2)
-    sum_terms(0)
-    leave(0)
     shared(D2)
     two_rows()
     start(term_copies(2))
     forward(L3A)
+    shared(L3B)
+    shared(L3C)
+    stage(three_begin)
+    neighbours_shared(L3A)
+    for j in (0, 1, 3):
+        three_rows(j)
+        start(quarter_copies(j))
     sum_terms(1)
     leave(1)
     finish(L3A)
-    for b in (L3A, L3B, L3C):
-        shared(b)
-    stage(three_rows)
-    start(term_copies(3))
     to_owner(0)
+    across(L3A, 3).wait_recv()
+    three_rows(2)
+    start(quarter_copies(2))
+    for j in (0, 1, 3):
+        leave_quarter(j)
     sum_terms(2)
     leave(2)
-    sum_terms(3)
-    leave(3)
+    leave_quarter(2)
     to_owner(1)
+    to_owner(3)
     to_owner(2)
-    to_owner(3)
-    for n in range(BATCHES):
-        received(owner_copies(n))
+    for n in (0, 1, 3, 2):
+        write(n)
 
     for b in range(9):
         settle(b)
@@ -665,8 +728,11 @@
         if n == 2:
             arrived(got_b.at[0:11], o_send.at[n])
         else:
-            arrived(mat.at[0 : (5, 5, 0, 3)[n], 0:5, 0, 0:32, 0:128], o_send.at[n])
-        for copy in term_copies(n) + owner_copies(n):
+            arrived(mat.at[0 : (5, 5, 0, 3)[n], 0:5, 0, 0:PART, 0:128], o_send.at[n])
+        for copy in (term_copies(n) if n < 3 else []) + owner_copies(n):
+            copy.wait_send()
+    for j in range(YN):
+        for copy in quarter_copies(j):
             copy.wait_send()
     for copy in diag_copies():
         copy.wait_send()
@@ -717,21 +783,25 @@
             pltpu.VMEM((384, W), BF16),
             pltpu.VMEM((256, W), BF16),
             pltpu.VMEM((128, W), BF16),
+            pltpu.VMEM((128, W), F32),
             pltpu.VMEM((384, W), BF16),
             pltpu.VMEM((256, W), BF16),
             pltpu.VMEM((128, W), BF16),
-            pltpu.VMEM((14, PART, COLS), F32),
-            pltpu.VMEM((14, PART, COLS), F32),
-            pltpu.VMEM((12, PART, COLS), F32),
-            pltpu.VMEM((8, PART, COLS), F32),
+            pltpu.VMEM((14, PART, COLS), BF16),
+            pltpu.VMEM((14, PART, COLS), BF16),
+            pltpu.VMEM((12, PART, COLS), BF16),
+            pltpu.VMEM((8, PART, COLS), BF16),
             pltpu.VMEM((XN - 1, 9, 2, 2, 2, 2, PART, 128), BF16),
-            pltpu.VMEM((9, 2, 2, 2, 2, PART, 128), F32),
+            pltpu.VMEM((9, 2, 2, 2, 2, PART, 128), BF16),
             pltpu.VMEM((15, XN, PART, COLS), BF16),
             pltpu.VMEM((XN - 1, 15, PART, COLS), BF16),
             pltpu.VMEM((15, PART, COLS), F32),
-            pltpu.VMEM((XN, 3, PART, COLS), F32),
-            pltpu.VMEM((XN, 2, 4, PART, COLS), F32),
-            pltpu.VMEM((5, PART, COLS), F32),
+            pltpu.VMEM((XN, 3, PART, COLS), BF16),
+            pltpu.VMEM((XN, 2, 4, PART, COLS), BF16),
+            pltpu.VMEM((5, PART, COLS), BF16),
+            pltpu.VMEM((XN, 3, PART, COLS), BF16),
+            pltpu.VMEM((XN, 2, 4, PART, COLS), BF16),
+            pltpu.VMEM((XN, 5, PART, COLS), BF16),
             pltpu.VMEM((XN - 1, 8, 128), F32),
             pltpu.VMEM((8, 128), F32),
             dma((4,)),
@@ -741,12 +811,12 @@
             dma((9, 2)),
             dma((9, 2)),
             dma((9,)),
-            dma((9, 2)),
+            dma((9, 3)),
             dma((3, 3)),
             dma((BATCHES,)),
             dma((BATCHES,)),
-            dma((BATCHES, XN - 1, 3)),
-            dma((BATCHES, XN - 1, 3)),
+            dma((BATCHES, XN - 1, 4)),
+            dma((BATCHES, XN - 1, 4)),
             dma((XN - 1, 2)),
             dma((XN - 1, 2)),
             dma((BATCHES, XN - 1, 3)),

time: 123 us -> 117 us (0.951)
  Pallas kernels: 117 us -> 111 us
    pallas_call x1, Pallas kernels: 117 us -> 111 us  [local(): pl.pallas_call(tree, out_shape=(jax.ShapeDtypeStruct((5, ROWS, COLS), F32...]
where the time goes in v4:
time: 117 us
  Pallas kernels  111 us (95%)
  local copies, waits for them, and re-layouts  4.19 us (4%)
  between operations  1.3 us (1%)
    pallas_call x1, Pallas kernels, local(): pl.pallas_call(tree, out_shape=(jax.ShapeDtypeStruct((5, ROWS, COLS), F32...  111 us
    unnamed x5, local copies, waits for them, and re-layouts  4.19 us

profile of v4, /device:TPU:1, one launch (start us, length us, event | category | flops | bytes accessed | tf_op | source)
XLA Modules:
  0.0 116.8 jit_solution(8108198279836531287)
XLA Ops:
  1.3 111.3 %shard_map.112 = (f32[5,64,256]{2,1,0:T(8,128)}, f32[1,3,64,256]{3,2,1,0:T(8,128)}, f32[2,4,64,256]{3,2,1,0:T(8,128)}) custom-call(bf16[2,64,256]{2,1,0:T(8,128)(2,1)} %bitcast.9, bf16[4,2,64,256]{3,2,1,0:T(8,128)(2,1)} %bitcast.8, bf16[8,3,64,256]{3,2,1,0:T(8,128)(2,1)} %bitcast.6, bf16[15,64,256]{2,1,0:T(8,128)(2,1)} %bitcast.7, s32[2,15]{1,0:T(2,128)} %bitcast.10, ...), custom_call_target="tpu_custom_call" | custom-call | tf_op jit(solution)/shard_map/pallas_call | solution.py:764
  112.6 0.0 copy-start
  112.6 1.8 %copy.16 = f32[5,64,256]{2,1,0:T(8,128)} copy(f32[5,64,256]{2,1,0:T(8,128)} %get-tuple-element.6) | data formatting | bytes 655360
  114.4 1.6 %copy.17 = f32[1,3,64,256]{3,2,1,0:T(8,128)} copy(f32[1,3,64,256]{3,2,1,0:T(8,128)} %get-tuple-element.7) | data formatting | bytes 393216
  116.0 0.0 copy-done
  116.0 0.8 copy.18
Async XLA Ops:
  112.6 3.4 %copy-start = (f32[2,4,64,256]{3,2,1,0:T(8,128)S(1)}, f32[2,4,64,256]{3,2,1,0:T(8,128)}, u32[]{:S(2)}) copy-start(f32[2,4,64,256]{3,2,1,0:T(8,128)} %get-tuple-element.8) | copy-start | bytes 1572868

commit v5 on v4

--- a/solution.py
+++ b/solution.py
@@ -79,9 +79,9 @@
     keep_two_ref,
     keep_three_ref,
     weight_ref,
-    top_ref,
-    out_two_ref,
-    out_three_ref,
+    full_two,
+    full_three,
+    full_top,
     one_ref,
     two_ref,
     three_ref,
@@ -110,9 +110,6 @@
     mine_two,
     mine_three,
     mine_top,
-    full_two,
-    full_three,
-    full_top,
     weights,
     own_weight,
     load_sem,
@@ -460,6 +457,10 @@
         for copy in copies:
             copy.start()
 
+    def sent(copies):
+        for copy in copies:
+            copy.wait_send()
+
     def received(copies):
         for copy in copies:
             copy.wait_recv()
@@ -578,7 +579,7 @@
     def owner_copies(n):
         copies = []
         for d in range(1, XN):
-            to = mod((pole + d), XN)
+            to = mod(pole + d, XN)
             pairs = [(mine_three.at[to, :, n], full_three.at[pole, :, n])]
             if n < 3:
                 pairs.append((mine_two.at[to, n], full_two.at[pole, n]))
@@ -597,18 +598,6 @@
             full_two[pole, n] = mine_two[pole, n]
         if n == 1:
             full_top[pole] = mine_top[...]
-
-    def write(n):
-        received(owner_copies(n))
-        for q in range(XN):
-            part = slice(q * PART, (q + 1) * PART)
-            for k in range(2):
-                out_three_ref[k, n, part] = full_three[q, k, n].astype(F32)
-            if n < 3:
-                out_two_ref[0, n, part] = full_two[q, n].astype(F32)
-            if n == 1:
-                for b in range(5):
-                    top_ref[b, part] = full_top[q, b].astype(F32)
 
     def stage(body):
         lax.fori_loop(0, 4, body, 0)
@@ -717,25 +706,30 @@
     leave(2)
     leave_quarter(2)
     to_owner(1)
+    for b in range(9):
+        settle(b)
+    sent(diag_copies())
     to_owner(3)
     to_owner(2)
+    for n in range(3):
+        sent(term_copies(n))
+    for j in range(YN):
+        sent(quarter_copies(j))
+    arrived(mat.at[0:5, 0:5, 0, 0:PART, 0:128], o_send.at[0])
+    arrived(mat.at[0:5, 0:5, 0, 0:PART, 0:128], o_send.at[1])
+    arrived(got_b.at[0:11], o_send.at[2])
+    arrived(mat.at[0:3, 0:5, 0, 0:PART, 0:128], o_send.at[3])
     for n in (0, 1, 3, 2):
-        write(n)
-
-    for b in range(9):
-        settle(b)
-    for n in range(BATCHES):
-        if n == 2:
-            arrived(got_b.at[0:11], o_send.at[n])
-        else:
-            arrived(mat.at[0 : (5, 5, 0, 3)[n], 0:5, 0, 0:PART, 0:128], o_send.at[n])
-        for copy in (term_copies(n) if n < 3 else []) + owner_copies(n):
-            copy.wait_send()
-    for j in range(YN):
-        for copy in quarter_copies(j):
-            copy.wait_send()
-    for copy in diag_copies():
-        copy.wait_send()
+        received(owner_copies(n))
+        sent(owner_copies(n))
+
+
+def write(two_ref, three_ref, top_ref, top_out, two_out, three_out):
+    for q in range(XN):
+        part = slice(q * PART, (q + 1) * PART)
+        top_out[:, part] = top_ref[q].astype(F32)
+        two_out[0, :, part] = two_ref[q].astype(F32)
+        three_out[:, :, part] = three_ref[q].astype(F32)
 
 
 VMEM = pl.BlockSpec(memory_space=pltpu.VMEM)
@@ -761,12 +755,12 @@
     diag = diag_inverse.reshape(15, ROWS, COLS)
 
     dma = pltpu.SemaphoreType.DMA
-    return pl.pallas_call(
+    parts = pl.pallas_call(
         tree,
         out_shape=(
-            jax.ShapeDtypeStruct((5, ROWS, COLS), F32),
-            jax.ShapeDtypeStruct((1, 3, ROWS, COLS), F32),
-            jax.ShapeDtypeStruct((2, 4, ROWS, COLS), F32),
+            jax.ShapeDtypeStruct((XN, 3, PART, COLS), BF16),
+            jax.ShapeDtypeStruct((XN, 2, 4, PART, COLS), BF16),
+            jax.ShapeDtypeStruct((XN, 5, PART, COLS), BF16),
         ),
         in_specs=[HBM] * 4 + [SMEM] * 5,
         out_specs=(VMEM, VMEM, VMEM),
@@ -799,9 +793,6 @@
             pltpu.VMEM((XN, 3, PART, COLS), BF16),
             pltpu.VMEM((XN, 2, 4, PART, COLS), BF16),
             pltpu.VMEM((5, PART, COLS), BF16),
-            pltpu.VMEM((XN, 3, PART, COLS), BF16),
-            pltpu.VMEM((XN, 2, 4, PART, COLS), BF16),
-            pltpu.VMEM((XN, 5, PART, COLS), BF16),
             pltpu.VMEM((XN - 1, 8, 128), F32),
             pltpu.VMEM((8, 128), F32),
             dma((4,)),
@@ -827,6 +818,17 @@
         ),
     )(one, two, three, diag, super_sizes.T, parents, keep_two, keep_three.T, pole_weight)
 
+    return pl.pallas_call(
+        write,
+        out_shape=(
+            jax.ShapeDtypeStruct((5, ROWS, COLS), F32),
+            jax.ShapeDtypeStruct((1, 3, ROWS, COLS), F32),
+            jax.ShapeDtypeStruct((2, 4, ROWS, COLS), F32),
+        ),
+        in_specs=[VMEM] * 3,
+        out_specs=(VMEM, VMEM, VMEM),
+    )(*parts)
+
 
 def solution(mesh):
     placed = (

time: 117 us -> 114 us (0.974)
  local copies, waits for them, and re-layouts: 4.19 us -> 0 us
  Pallas kernels: 111 us -> 113 us
    unnamed x5 -> x0, local copies, waits for them, and re-layouts: 4.19 us -> none
    pallas_call x1 -> x2, Pallas kernels: 111 us -> 113 us  [the longest x1 111 us: local(): pl.pallas_call(tree, out_shape=(jax.ShapeDtypeStruct((XN, 3, PART, COLS),...]
where the time goes in v5:
time: 114 us
  Pallas kernels  113 us (99%)
  between operations  1.29 us (1%)
    pallas_call x1, Pallas kernels, local(): pl.pallas_call(tree, out_shape=(jax.ShapeDtypeStruct((XN, 3, PART, COLS),...  111 us

profile of v5, /device:TPU:1, one launch (start us, length us, event | category | flops | bytes accessed | tf_op | source)
XLA Modules:
  0.0 114.3 jit_solution(6386828829928555018)
XLA Ops:
  1.3 111.0 %shard_map.112 = (bf16[4,3,16,256]{3,2,1,0:T(8,128)(2,1)}, bf16[4,2,4,16,256]{4,3,2,1,0:T(8,128)(2,1)}, bf16[4,5,16,256]{3,2,1,0:T(8,128)(2,1)}) custom-call(bf16[2,64,256]{2,1,0:T(8,128)(2,1)} %bitcast.9, bf16[4,2,64,256]{3,2,1,0:T(8,128)(2,1)} %bitcast.8, bf16[8,3,64,256]{3,2,1,0:T(8,128)(2,1)} %bitcast.6, bf16[15,64,256]{2,1,0:T(8,128)(2,1)} %bitcast.7, ...), custom_call_target="tpu_custom_call" | custom-call | tf_op jit(solution)/shard_map/pallas_call | solution.py:758
  112.3 2.0 %shard_map.113 = (f32[5,64,256]{2,1,0:T(8,128)}, f32[1,3,64,256]{3,2,1,0:T(8,128)}, f32[2,4,64,256]{3,2,1,0:T(8,128)}) custom-call(bf16[4,3,16,256]{3,2,1,0:T(8,128)(2,1)} %get-tuple-element.6.two_ref, bf16[4,2,4,16,256]{4,3,2,1,0:T(8,128)(2,1)} %get-tuple-element.7.three_ref, bf16[4,5,16,256]{3,2,1,0:T(8,128)(2,1)} %get-tuple-element.8.top_ref), custom_call_target="tpu_custom_call" | custom-call | tf_op jit(solution)/shard_map/pallas_call | solution.py:821

commit v6 on v5

--- a/solution.py
+++ b/solution.py
@@ -696,10 +696,10 @@
     sum_terms(1)
     leave(1)
     finish(L3A)
-    to_owner(0)
     across(L3A, 3).wait_recv()
     three_rows(2)
     start(quarter_copies(2))
+    to_owner(0)
     for j in (0, 1, 3):
         leave_quarter(j)
     sum_terms(2)

time: 114 us -> 114 us (level)
  no operation moved by 1% of the time
where the time goes in v6:
time: 114 us
  Pallas kernels  112 us (98%)
  between operations  1.29 us (1%)
    pallas_call x1, Pallas kernels, local(): pl.pallas_call(tree, out_shape=(jax.ShapeDtypeStruct((XN, 3, PART, COLS),...  110 us

profile of v6, /device:TPU:1, one launch (start us, length us, event | category | flops | bytes accessed | tf_op | source)
XLA Modules:
  0.0 113.7 jit_solution(543222492020160787)
XLA Ops:
  1.3 110.4 %shard_map.112 = (bf16[4,3,16,256]{3,2,1,0:T(8,128)(2,1)}, bf16[4,2,4,16,256]{4,3,2,1,0:T(8,128)(2,1)}, bf16[4,5,16,256]{3,2,1,0:T(8,128)(2,1)}) custom-call(bf16[2,64,256]{2,1,0:T(8,128)(2,1)} %bitcast.9, bf16[4,2,64,256]{3,2,1,0:T(8,128)(2,1)} %bitcast.8, bf16[8,3,64,256]{3,2,1,0:T(8,128)(2,1)} %bitcast.6, bf16[15,64,256]{2,1,0:T(8,128)(2,1)} %bitcast.7, ...), custom_call_target="tpu_custom_call" | custom-call | tf_op jit(solution)/shard_map/pallas_call | solution.py:758
  111.7 2.0 %shard_map.113 = (f32[5,64,256]{2,1,0:T(8,128)}, f32[1,3,64,256]{3,2,1,0:T(8,128)}, f32[2,4,64,256]{3,2,1,0:T(8,128)}) custom-call(bf16[4,3,16,256]{3,2,1,0:T(8,128)(2,1)} %get-tuple-element.6.two_ref, bf16[4,2,4,16,256]{4,3,2,1,0:T(8,128)(2,1)} %get-tuple-element.7.three_ref, bf16[4,5,16,256]{3,2,1,0:T(8,128)(2,1)} %get-tuple-element.8.top_ref), custom_call_target="tpu_custom_call" | custom-call | tf_op jit(solution)/shard_map/pallas_call | solution.py:821
